TPU v7x, 256 devices: a whole 4x4x8 slice. The times are simulated.
256 devices in a mesh: var: 8 (over x, z_hi), seq: 32 (over z_lo, y, core).
Axes of the slice: x: 4, y: 4, z: 8 (z_hi: 2, z_lo: 4; z = z_hi * 4 + z_lo), core: 2. Of those that a mesh axis runs over, the one named last changes fastest.
Arguments:
- patches: bfloat16 [96, 16, 8192], P(None, None, 'seq'), may hold values from -6 to 6
- embed_weight: bfloat16 [96, 16, 4096], P(None, None, 'var'), may hold values from -1.5 to 1.5
- var_embed: bfloat16 [96, 4096], P(None, 'var'), may hold values from -3 to 3
- key_query: bfloat16 [4096, 32], P('var'), may hold values from -0.1875 to 0.1875
- var_mask: int32 [96], replicated, may hold values from 0 to 1, as said below
- value_weight: bfloat16 [4096, 32, 128], P('var', 'seq'), may hold values from -0.1875 to 0.1875
- out_weight: bfloat16 [4096, 4096], P('var', 'seq'), may hold values from -0.1875 to 0.1875
- out_bias: bfloat16 [4096], P('var'), may hold values from -3 to 3
Outputs:
- aggregated_tokens: bfloat16 [8192, 4096], P('seq', 'var')
Inputs may be any that keep to these rules, and one draw needn't show every extreme that they name: `var_mask`: exactly 91 entries are 1.
All inputs are finite; a program needn't handle non-finite values.
Results may differ from a plain program's by a relative error of at most 0.025.
Values may be sent and summed in bfloat16 or wider, within the bound.
A program may use at most 128 MiB of HBM per device.

v0:
```python
import jax
import jax.numpy as jnp
from jax import lax
from jax.sharding import PartitionSpec as P


def normalize(scores, var_mask):
    raised = jnp.exp(scores) * var_mask.astype(jnp.float32)[None, :, None]
    return (raised / jnp.sum(raised, axis=1, keepdims=True)).astype(jnp.bfloat16)


def local(
    patches, embed_weight, var_embed, key_query, var_mask, value_weight, out_weight, out_bias
):
    embedded = jnp.einsum("vpt,vpd->vtd", patches, embed_weight, preferred_element_type=jnp.float32)
    embedded = (embedded + var_embed.astype(jnp.float32)[:, None, :]).astype(jnp.bfloat16)
    partial_scores = jnp.einsum(
        "vtd,dh->hvt", embedded, key_query, preferred_element_type=jnp.float32
    )
    scores = lax.psum(partial_scores, "var")
    attention = normalize(scores, var_mask)
    pooled = jnp.einsum(
        "hvt,vtd->htd", attention, embedded, preferred_element_type=jnp.float32
    ).astype(jnp.bfloat16)
    tok_rows = pooled.shape[1]
    partial_heads = jnp.einsum(
        "htd,dhe->the",
        pooled,
        lax.all_gather(value_weight, "seq", axis=1, tiled=True),
        preferred_element_type=jnp.float32,
    )
    partial_values = partial_heads.reshape(tok_rows, -1)
    projected = lax.psum_scatter(
        partial_values.astype(jnp.bfloat16), "var", scatter_dimension=1, tiled=True
    )
    partial_out = jnp.dot(
        projected,
        lax.all_gather(out_weight, "seq", axis=1, tiled=True),
        preferred_element_type=jnp.float32,
    )
    summed = lax.psum_scatter(
        partial_out.astype(jnp.bfloat16), "var", scatter_dimension=1, tiled=True
    ).astype(jnp.float32)
    return (summed + out_bias.astype(jnp.float32)[None, :]).astype(jnp.bfloat16)


def solution(mesh):
    placed = (
        P(None, None, "seq"),
        P(None, None, "var"),
        P(None, "var"),
        P("var", None),
        P(),
        P("var", "seq", None),
        P("var", "seq"),
        P("var"),
    )
    return jax.shard_map(
        local, mesh=mesh, in_specs=placed, out_specs=P("seq", "var"), check_vma=False
    )
```

profile of v0, /device:TPU:1, one launch (start us, length us, event | category | flops | bytes accessed | tf_op | source)
XLA Modules:
  0.0 571.7 jit_solution(7919094501001668481)
XLA Ops:
  7.4 0.0 copy-start
  7.4 0.0 all-reduce.2.cloned.1.call-start
  7.4 1.0 convert_element_type.39
  8.4 0.4 copy-done
  8.8 0.0 copy-start.2
  8.8 12.9 %add_convert_fusion = bf16[96,256,512]{2,1,0:T(8,128)(2,1)} fusion(f32[96,512]{1,0:T(8,128)S(1)} %convert_element_type.39, bf16[96,16,256]{2,1,0:T(8,128)(2,1)} %param.8, bf16[96,16,512]{2,1,0:T(8,128)(2,1)S(1)} %copy-done), kind=kOutput, calls=%fused_computation | convolution fusion | flops 427819008 | bytes 27721728 | tf_op jit(solution)/shard_map/vpt,vpd->vtd/dot_general | solution.py:15
  21.7 0.0 copy-done.2
  21.7 0.0 copy-start.4
  21.7 17.3 %convolution_bitcast_fusion = f32[32,96,256]{2,0,1:T(8,128)} fusion(bf16[96,256,512]{2,1,0:T(8,128)(2,1)} %add_convert_fusion, bf16[512,32]{0,1:T(8,128)(2,1)S(1)} %copy-done.2), kind=kOutput, calls=%fused_computation.10 | convolution fusion | flops 805306368 | bytes 28344320 | tf_op jit(solution)/shard_map/vtd,dh->hvt/dot_general | solution.py:17
  39.0 0.0 all-reduce.2.cloned.1.call-update
  39.0 0.0 all-gather.3.cloned.1.call-start
  39.1 0.5 all-gather.3.cloned.1.call-update
  39.6 0.0 all-gather.5.cloned.1.call-start
  39.7 0.5 all-gather.5.cloned.1.call-update
  40.2 0.0 reduce-scatter.3.cloned.1.call-start
  40.3 0.0 copy-done.4
  40.3 287.8 %all-reduce.2.cloned.1.call-done = f32[32,96,256]{2,0,1:T(8,128)} async-done(((f32[32,96,256]{2,0,1:T(8,128)}), f32[32,96,256]{2,0,1:T(8,128)}) %all-reduce.2.cloned.1.call-update) | async-done | bytes 3145744 | tf_op jit(solution)/shard_map/psum | solution.py:20
  328.1 0.0 copy-start.1
  328.1 2.5 fusion.5
  330.6 0.3 copy-done.1
  330.9 0.5 divide_convert_fusion
  331.5 3.8 copy.12
  335.3 29.9 %fusion = bf16[256,512,32]{1,2,0:T(8,128)(2,1)} fusion(bf16[32,96,256]{1,0,2:T(8,128)(2,1)} %copy.12, bf16[96,256,512]{2,1,0:T(8,128)(2,1)} %add_convert_fusion), kind=kOutput, calls=%fused_computation.1 | convolution fusion | flops 805306368 | bytes 35127296 | tf_op jit(solution)/shard_map/hvt,vtd->htd/dot_general | solution.py:22
  365.2 0.0 all-gather.3.cloned.1.call-done
  365.2 11.1 %fusion.6 = bf16[32,256,128]{1,2,0:T(8,128)(2,1)} fusion(bf16[512,32,128]{2,0,1:T(8,128)(2,1)} %all-gather.3.cloned.1.call-done, bf16[256,512,32]{1,2,0:T(8,128)(2,1)} %fusion), kind=kOutput, calls=%fused_computation.11 | convolution fusion | flops 1074790400 | bytes 14680064 | tf_op jit(solution)/shard_map/htd,dhe->the/dot_general | solution.py:26
  376.3 0.0 reduce-scatter.3.cloned.1.call-update
  376.4 0.0 copy-start.3
  376.4 0.0 reduce-scatter.5.cloned.1.call-start
  376.4 43.9 %all-gather.5.cloned.1.call-done = bf16[512,4096]{1,0:T(8,128)(2,1)} async-done(((bf16[512,128]{1,0:T(8,128)(2,1)}), bf16[512,4096]{1,0:T(8,128)(2,1)}) %all-gather.5.cloned.1.call-update) | async-done | bytes 4194320 | tf_op jit(solution)/shard_map/all_gather | solution.py:38
  420.3 46.6 %reduce-scatter.3.cloned.1.call-done = bf16[256,512]{0,1:T(8,128)(2,1)} async-done(((bf16[256,4096]{0,1:T(8,128)(2,1)}), bf16[256,512]{0,1:T(8,128)(2,1)}) %reduce-scatter.3.cloned.1.call-update) | async-done | bytes 262160 | tf_op jit(solution)/shard_map/reduce_scatter | solution.py:33
  466.9 4.9 convolution_convert_fusion
  471.8 0.0 reduce-scatter.5.cloned.1.call-update
  471.8 0.0 copy-done.3
  471.9 91.0 %reduce-scatter.5.cloned.1.call-done = bf16[256,512]{1,0:T(8,128)(2,1)} async-done(((bf16[256,4096]{1,0:T(8,128)(2,1)}), bf16[256,512]{1,0:T(8,128)(2,1)}) %reduce-scatter.5.cloned.1.call-update) | async-done | bytes 262160 | tf_op jit(solution)/shard_map/reduce_scatter | solution.py:41
  562.9 1.7 add_convert_fusion.1
  (2 shorter events, 0.0 us)
Async XLA Ops:
  7.4 1.5 copy-start
  7.4 320.7 %all-reduce.2.cloned.1.call-start = ((), (), s32[]{:S(2)}) async-start(), calls=%async_computation.2 | async-start | bytes 6291456 | tf_op jit(solution)/shard_map/psum | solution.py:20
  8.8 12.9 %copy-start.2 = (bf16[512,32]{0,1:T(8,128)(2,1)S(1)}, bf16[512,32]{0,1:T(8,128)(2,1)}, u32[]{:S(2)}) copy-start(bf16[512,32]{0,1:T(8,128)(2,1)} %param.11) | copy-start | bytes 98308
  21.7 18.5 %copy-start.4 = (s32[96]{0:T(128)S(1)}, s32[96]{0:T(128)}, u32[]{:S(2)}) copy-start(s32[96]{0:T(128)} %param.12) | copy-start | bytes 1156
  39.0 326.1 %all-gather.3.cloned.1.call-start = ((), (), s32[]{:S(2)}) async-start(), calls=%async_computation.3 | async-start | bytes 4325376 | tf_op jit(solution)/shard_map/all_gather | solution.py:29
  39.6 380.7 %all-gather.5.cloned.1.call-start = ((), (), s32[]{:S(2)}) async-start(), calls=%async_computation.5 | async-start | bytes 4325376 | tf_op jit(solution)/shard_map/all_gather | solution.py:38
  40.2 426.7 %reduce-scatter.3.cloned.1.call-start = ((), (), s32[]{:S(2)}) async-start(), calls=%async_computation.4 | async-start | bytes 2359296 | tf_op jit(solution)/shard_map/reduce_scatter | solution.py:33
  328.1 2.8 copy-start.1
  376.4 95.5 %copy-start.3 = (bf16[512]{0:T(512)(128)(2,1)S(1)}, bf16[512]{0:T(512)(128)(2,1)}, u32[]{:S(2)}) copy-start(bf16[512]{0:T(512)(128)(2,1)} %param.15) | copy-start | bytes 3076
  376.4 186.5 %reduce-scatter.5.cloned.1.call-start = ((), (), s32[]{:S(2)}) async-start(), calls=%async_computation.6 | async-start | bytes 2359296 | tf_op jit(solution)/shard_map/reduce_scatter | solution.py:41
Sparse Core Ops, SparseCore 0:
  39.2 288.8 all-reduce.1
  376.5 90.4 reduce-scatter.2
  472.0 90.8 reduce-scatter.4
Sparse Core Ops, SparseCore 1:
  41.4 295.5 all-gather.2
  338.7 81.6 all-gather.4
where the time goes:
time: 573 us; the launch traced here: 572 us
  waiting for transfers between devices  470 us (82%)
  matrix products  76.2 us (13%)
  between operations  14.6 us (3%)
  other arithmetic  5.75 us (1%)
    psum x1, waiting for transfers between devices, local(): scores = lax.psum(partial_scores, 'var')  288 us
    reduce_scatter x1, waiting for transfers between devices, local(): lax.psum_scatter(partial_out.astype(jnp.bfloat16), 'var', scatter_dimensi...  91 us
    reduce_scatter x1, waiting for transfers between devices, local(): lax.psum_scatter(partial_values.astype(jnp.bfloat16), 'var', scatter_dime...  46.6 us
    all_gather x1, waiting for transfers between devices, local(): lax.all_gather(out_weight, 'seq', axis=1, tiled=True)  43.9 us
    dot_general x1, matrix products, local(): jnp.einsum('hvt,vtd->htd', attention, embedded, preferred_element_type=jn...  29.9 us
    dot_general x1, matrix products, local(): jnp.einsum('vtd,dh->hvt', embedded, key_query, preferred_element_type=jnp...  17.3 us
    dot_general x1, matrix products, local(): jnp.einsum('vpt,vpd->vtd', patches, embed_weight, preferred_element_type=...  12.9 us
  transfers between devices with their start and end apart: 5, of which 4 were waited for; matrix products, arithmetic and copies ran while one was open for 8% of the time, Pallas kernels for 0%

commit v1 on v0

--- a/solution.py
+++ b/solution.py
@@ -12,13 +12,30 @@
 def local(
     patches, embed_weight, var_embed, key_query, var_mask, value_weight, out_weight, out_bias
 ):
+    folded_query = lax.psum(
+        jnp.concatenate(
+            [
+                jnp.einsum(
+                    "vpd,dh->vph", embed_weight, key_query, preferred_element_type=jnp.float32
+                ),
+                jnp.dot(var_embed, key_query, preferred_element_type=jnp.float32)[:, None, :],
+            ],
+            axis=1,
+        ),
+        "var",
+    )
+    scores = (
+        jnp.einsum(
+            "vph,vpt->hvt",
+            folded_query[:, :16],
+            patches.astype(jnp.float32),
+            precision=lax.Precision.HIGHEST,
+        )
+        + folded_query[:, 16].T[:, :, None]
+    )
+    attention = normalize(scores, var_mask)
     embedded = jnp.einsum("vpt,vpd->vtd", patches, embed_weight, preferred_element_type=jnp.float32)
     embedded = (embedded + var_embed.astype(jnp.float32)[:, None, :]).astype(jnp.bfloat16)
-    partial_scores = jnp.einsum(
-        "vtd,dh->hvt", embedded, key_query, preferred_element_type=jnp.float32
-    )
-    scores = lax.psum(partial_scores, "var")
-    attention = normalize(scores, var_mask)
     pooled = jnp.einsum(
         "hvt,vtd->htd", attention, embedded, preferred_element_type=jnp.float32
     ).astype(jnp.bfloat16)

time: 573 us -> 409 us (0.71)
  waiting for transfers between devices: 470 us -> 320 us
  matrix products: 76.2 us -> 63.3 us
    psum x1, waiting for transfers between devices: 288 us -> 131 us  [local(): lax.psum(jnp.concatenate([jnp.einsum('vpd,dh->vph', embed_weight, key_que...]
    reduce_scatter x1, waiting for transfers between devices: 46.6 us -> 77.8 us  [local(): lax.psum_scatter(partial_values.astype(jnp.bfloat16), 'var', scatter_dime...]
    all_gather x1, waiting for transfers between devices: 43.9 us -> 18.3 us  [local(): lax.all_gather(out_weight, 'seq', axis=1, tiled=True)]
    dot_general x1 -> x3, matrix products: 17.3 us -> 5.59 us  [the longest x1 3.25 us: local(): jnp.einsum('vph,vpt->hvt', folded_query[:, :16], patches.astype(jnp.float...]
  transfers between devices with their start and end apart: 5 -> 5, of which waited for: 4 -> 4; matrix products, arithmetic and copies ran while one was open for 8% -> 15% of each run, Pallas kernels for 0% -> 0%
where the time goes in v1:
time: 409 us; the launch traced here: 408 us
  waiting for transfers between devices  320 us (78%)
  matrix products  63.3 us (15%)
  between operations  14.7 us (4%)
  local copies, waits for them, and re-layouts  6.02 us (1%)
    psum x1, waiting for transfers between devices, local(): lax.psum(jnp.concatenate([jnp.einsum('vpd,dh->vph', embed_weight, key_que...  131 us
    reduce_scatter x1, waiting for transfers between devices, local(): lax.psum_scatter(partial_out.astype(jnp.bfloat16), 'var', scatter_dimensi...  91.2 us
    reduce_scatter x1, waiting for transfers between devices, local(): lax.psum_scatter(partial_values.astype(jnp.bfloat16), 'var', scatter_dime...  77.8 us
    dot_general x1, matrix products, local(): jnp.einsum('hvt,vtd->htd', attention, embedded, preferred_element_type=jn...  30 us
    all_gather x1, waiting for transfers between devices, local(): lax.all_gather(out_weight, 'seq', axis=1, tiled=True)  18.3 us
    dot_general x1, matrix products, local(): jnp.einsum('vpt,vpd->vtd', patches, embed_weight, preferred_element_type=...  11.7 us
    dot_general x1, matrix products, local(): jnp.einsum('htd,dhe->the', pooled, lax.all_gather(value_weight, 'seq', ax...  11.1 us
  transfers between devices with their start and end apart: 5, of which 4 were waited for; matrix products, arithmetic and copies ran while one was open for 15% of the time, Pallas kernels for 0%

profile of v1, /device:TPU:1, one launch (start us, length us, event | category | flops | bytes accessed | tf_op | source)
XLA Modules:
  0.0 407.8 jit_solution(109429828332832161)
XLA Ops:
  7.4 0.0 copy-start
  7.4 0.0 copy-start.2
  7.4 0.0 copy-start.4
  7.4 0.0 copy-start.1
  7.4 0.0 all-reduce.2.cloned.1.call-start
  7.4 1.4 copy-done
  8.8 1.3 fusion.14
  10.1 1.0 fusion.16
  11.1 1.1 pad_maximum_fusion
  12.3 0.0 all-reduce.2.cloned.1.call-update
  12.3 0.0 all-gather.3.cloned.1.call-start
  12.3 0.5 all-gather.3.cloned.1.call-update
  12.9 0.0 all-gather.5.cloned.1.call-start
  12.9 0.5 all-gather.5.cloned.1.call-update
  13.4 0.0 reduce-scatter.3.cloned.1.call-start
  13.5 0.0 copy-done.2
  13.5 0.0 copy-done.4
  13.5 0.0 copy-done.1
  13.6 11.7 %add_convert_fusion = bf16[96,256,512]{2,1,0:T(8,128)(2,1)} fusion(f32[96,512]{1,0:T(8,128)S(1)} %convert_element_type.40, bf16[96,16,256]{2,1,0:T(8,128)(2,1)S(1)} %copy-done.1, bf16[96,16,512]{2,1,0:T(8,128)(2,1)S(1)} %copy-done), kind=kOutput, calls=%fused_computation | convolution fusion | flops 427819008 | bytes 27721728 | tf_op jit(solution)/shard_map/vpt,vpd->vtd/dot_general | solution.py:37
  25.3 131.5 %all-reduce.2.cloned.1.call-done = f32[96,17,32]{2,1,0:T(8,128)} async-done(((f32[96,17,32]{2,1,0:T(8,128)}), f32[96,17,32]{2,1,0:T(8,128)}) %all-reduce.2.cloned.1.call-update) | async-done | bytes 208912 | tf_op jit(solution)/shard_map/psum | solution.py:15
  156.8 1.0 slice.9
  157.8 3.3 fusion.8
  161.0 0.9 divide_convert_fusion
  161.9 3.6 copy.16
  165.5 30.0 %convert_bitcast_fusion = bf16[32,256,512]{2,0,1:T(8,128)(2,1)} fusion(bf16[32,96,256]{1,0,2:T(8,128)(2,1)} %copy.16, bf16[96,256,512]{2,1,0:T(8,128)(2,1)} %add_convert_fusion), kind=kOutput, calls=%fused_computation.5 | convolution fusion | flops 809500672 | bytes 35127296 | tf_op jit(solution)/shard_map/hvt,vtd->htd/dot_general | solution.py:39
  195.5 0.0 all-gather.3.cloned.1.call-done
  195.5 11.1 %fusion.9 = bf16[32,256,128]{1,2,0:T(8,128)(2,1)} fusion(bf16[512,32,128]{2,0,1:T(8,128)(2,1)} %all-gather.3.cloned.1.call-done, bf16[32,256,512]{2,0,1:T(8,128)(2,1)} %convert_bitcast_fusion), kind=kOutput, calls=%fused_computation.12 | convolution fusion | flops 1074790400 | bytes 14680064 | tf_op jit(solution)/shard_map/htd,dhe->the/dot_general | solution.py:43
  206.7 0.0 reduce-scatter.3.cloned.1.call-update
  206.7 0.0 copy-start.3
  206.7 0.0 reduce-scatter.5.cloned.1.call-start
  206.8 18.3 %all-gather.5.cloned.1.call-done = bf16[512,4096]{1,0:T(8,128)(2,1)} async-done(((bf16[512,128]{1,0:T(8,128)(2,1)}), bf16[512,4096]{1,0:T(8,128)(2,1)}) %all-gather.5.cloned.1.call-update) | async-done | bytes 4194320 | tf_op jit(solution)/shard_map/all_gather | solution.py:55
  225.1 77.8 %reduce-scatter.3.cloned.1.call-done = bf16[256,512]{0,1:T(8,128)(2,1)} async-done(((bf16[256,4096]{0,1:T(8,128)(2,1)}), bf16[256,512]{0,1:T(8,128)(2,1)}) %reduce-scatter.3.cloned.1.call-update) | async-done | bytes 262160 | tf_op jit(solution)/shard_map/reduce_scatter | solution.py:50
  302.8 4.9 %convolution_convert_fusion = bf16[256,4096]{1,0:T(8,128)(2,1)} fusion(bf16[256,512]{0,1:T(8,128)(2,1)} %reduce-scatter.3.cloned.1.call-done, bf16[512,4096]{1,0:T(8,128)(2,1)} %all-gather.5.cloned.1.call-done), kind=kOutput, calls=%fused_computation.6 | convolution fusion | flops 1074790400 | bytes 6553600 | tf_op jit(solution)/shard_map/dot_general | solution.py:53
  307.7 0.0 reduce-scatter.5.cloned.1.call-update
  307.8 0.0 copy-done.3
  307.8 91.2 %reduce-scatter.5.cloned.1.call-done = bf16[256,512]{1,0:T(8,128)(2,1)} async-done(((bf16[256,4096]{1,0:T(8,128)(2,1)}), bf16[256,512]{1,0:T(8,128)(2,1)}) %reduce-scatter.5.cloned.1.call-update) | async-done | bytes 262160 | tf_op jit(solution)/shard_map/reduce_scatter | solution.py:58
  399.0 1.7 add_convert_fusion.1
  (3 shorter events, 0.0 us)
Async XLA Ops:
  7.4 1.4 copy-start
  7.4 6.1 %copy-start.2 = (bf16[96,512]{1,0:T(8,128)(2,1)S(1)}, bf16[96,512]{1,0:T(8,128)(2,1)}, u32[]{:S(2)}) copy-start(bf16[96,512]{1,0:T(8,128)(2,1)} %param.10) | copy-start | bytes 294916
  7.4 6.2 %copy-start.4 = (s32[96]{0:T(128)S(1)}, s32[96]{0:T(128)}, u32[]{:S(2)}) copy-start(s32[96]{0:T(128)} %param.12) | copy-start | bytes 1156
  7.4 6.2 %copy-start.1 = (bf16[96,16,256]{2,1,0:T(8,128)(2,1)S(1)}, bf16[96,16,256]{2,1,0:T(8,128)(2,1)}, u32[]{:S(2)}) copy-start(bf16[96,16,256]{2,1,0:T(8,128)(2,1)} %param.8) | copy-start | bytes 2359300
  7.4 149.4 %all-reduce.2.cloned.1.call-start = ((), (), s32[]{:S(2)}) async-start(), calls=%async_computation.2 | async-start | bytes 2359296 | tf_op jit(solution)/shard_map/psum | solution.py:15
  12.3 183.3 %all-gather.3.cloned.1.call-start = ((), (), s32[]{:S(2)}) async-start(), calls=%async_computation.3 | async-start | bytes 4325376 | tf_op jit(solution)/shard_map/all_gather | solution.py:46
  12.9 212.2 %all-gather.5.cloned.1.call-start = ((), (), s32[]{:S(2)}) async-start(), calls=%async_computation.5 | async-start | bytes 4325376 | tf_op jit(solution)/shard_map/all_gather | solution.py:55
  13.4 289.4 %reduce-scatter.3.cloned.1.call-start = ((), (), s32[]{:S(2)}) async-start(), calls=%async_computation.4 | async-start | bytes 2359296 | tf_op jit(solution)/shard_map/reduce_scatter | solution.py:50
  206.7 101.1 %copy-start.3 = (bf16[512]{0:T(512)(128)(2,1)S(1)}, bf16[512]{0:T(512)(128)(2,1)}, u32[]{:S(2)}) copy-start(bf16[512]{0:T(512)(128)(2,1)} %param.15) | copy-start | bytes 3076
  206.7 192.3 %reduce-scatter.5.cloned.1.call-start = ((), (), s32[]{:S(2)}) async-start(), calls=%async_computation.6 | async-start | bytes 2359296 | tf_op jit(solution)/shard_map/reduce_scatter | solution.py:58
Sparse Core Ops, SparseCore 0:
  12.4 144.3 all-reduce.1
  206.8 95.9 reduce-scatter.2
  307.9 91.0 reduce-scatter.4
Sparse Core Ops, SparseCore 1:
  14.6 110.6 all-gather.2
  127.1 98.0 all-gather.4

commit v2 on v0

v2 whole, which is shorter than its diff:
```python
import jax
import jax.numpy as jnp
from jax import lax
from jax.experimental import pallas as pl
from jax.experimental.pallas import tpu as pltpu
from jax.sharding import PartitionSpec as P

MESH = pl.DeviceIdType.MESH
F32 = jnp.float32
BF16 = jnp.bfloat16
VARS, PIX, TOK = 96, 16, 256
ROWS = VARS * PIX
DEPTH = ROWS + 128
CHUNK = 256
VAR_CHUNK = CHUNK // PIX
HEADS_DEV = 4
COLS = 512


def iota(shape, dim):
    return lax.broadcasted_iota(jnp.int32, shape, dim)


def kernel(
    patches,
    weight,
    embed,
    left_side,
    mask,
    out_weight,
    bias,
    out,
    o_all,
    u_all,
    table_out,
    table_in,
    u_part,
    u_in_x,
    u_mid,
    u_in_z,
    embed_pad,
    table,
    scores,
    attention,
    weighted,
    heads,
    total,
    o_send,
    o_recv,
    u_send,
    u_recv,
    o_swap,
    t_send,
    t_recv,
    x_send,
    x_recv,
    z_send,
    z_recv,
    p_send,
    p_recv,
):
    me = lax.axis_index("var")
    seat = lax.axis_index("seq")
    x, half = lax.div(me, 2), lax.rem(me, 2)
    zlo, y, core = lax.div(seat, 8), lax.rem(lax.div(seat, 2), 4), lax.rem(seat, 2)

    def place(dz, dy, dc=0):
        return (
            lax.rem(zlo + dz + 4, 4) * 8 + lax.rem(y + dy + 4, 4) * 2 + lax.rem(core + dc, 2)
        )

    def remote(src, dst, send, recv, device):
        return pltpu.make_async_remote_copy(
            src_ref=src,
            dst_ref=dst,
            send_sem=send,
            recv_sem=recv,
            device_id=device,
            device_id_type=MESH,
        )

    sent = []

    def go(*args):
        copy = remote(*args)
        copy.start()
        sent.append(copy)

    class Gather:
        def __init__(self, buf, send, recv):
            self.buf, self.send, self.recv, self.count = buf, send, recv, 0

        def push(self, piece, target):
            go(
                self.buf.at[piece],
                self.buf.at[piece],
                self.send.at[self.count],
                self.recv.at[piece],
                (me, target),
            )
            self.count += 1

        def arrive(self, piece):
            remote(
                self.buf.at[piece],
                self.buf.at[piece],
                self.send.at[0],
                self.recv.at[piece],
                (me, seat),
            ).wait_recv()

        def own(self):
            for dz in (1, 2, 3):
                self.push(seat, place(dz, 0))
            self.sides(seat)

        def sides(self, piece):
            self.push(piece, place(0, 1))
            self.push(piece, place(0, -1))
            self.push(piece, place(0, 0, 1))

        def line(self):
            for dz in (1, 2, 3):
                piece = place(-dz, 0)
                self.arrive(piece)
                self.sides(piece)

        def ring(self):
            for dz in range(4):
                left, right = place(-dz, -1), place(-dz, 1)
                self.arrive(left)
                if dz % 2 == 0:
                    self.push(left, place(0, 1))
                self.push(left, place(0, 0, 1))
                self.arrive(right)
                if dz % 2 == 1:
                    self.push(right, place(0, -1))
                self.push(right, place(0, 0, 1))

        def far(self):
            for dz in range(4):
                piece = place(-dz, 2)
                self.arrive(piece)
                self.push(piece, place(0, 0, 1))

        def sibling(self):
            for dz in range(4):
                for dy in (0, -1, 1, 2):
                    self.arrive(place(-dz, dy, 1))

    o_gather = Gather(o_all, o_send, o_recv)
    u_gather = Gather(u_all, u_send, u_recv)

    plane, slot = lax.div(seat, 4), lax.rem(seat, 4)
    stays = plane == me
    swap = remote(
        out_weight,
        o_all.at[me * 4 + slot],
        o_swap.at[0],
        o_swap.at[1],
        (plane, me * 4 + slot),
    )

    @pl.when(jnp.logical_not(stays))
    def _():
        swap.start()

    @pl.when(stays)
    def _():
        o_all[seat] = out_weight[...]

    embed_pad[...] = jnp.zeros_like(embed_pad)
    embed_pad[0:VARS] = embed[...]
    for part in range(4):
        wide = 512 if part < 3 else 128
        rhs = weight[part * 512 : part * 512 + 512] if part < 3 else embed_pad[...]
        both = lax.dot_general(
            left_side[...], rhs, (((1,), (1,)), ((), ())), preferred_element_type=F32
        )
        for group in range(8):
            u_part[group, :, part * 512 : part * 512 + wide] = both[
                group * 16 : group * 16 + 16
            ].astype(BF16)
            table_out[group, :, part * 512 : part * 512 + wide] = both[
                128 + group * 4 : 132 + group * 4
            ]
    for dx in (1, 2, 3):
        target = lax.rem(x + dx, 4)
        go(
            u_part.at[pl.ds(target * 2, 2)],
            u_in_x.at[dx - 1],
            x_send.at[dx - 1],
            x_recv.at[dx - 1],
            (target * 2 + half, seat),
        )
    for step in range(1, 8):
        target = lax.rem(me + step, 8)
        go(
            table_out.at[target],
            table_in.at[step - 1],
            t_send.at[step - 1],
            t_recv.at[step - 1],
            (target, seat),
        )

    @pl.when(jnp.logical_not(stays))
    def _():
        swap.wait_recv()

    o_gather.own()

    for dx in (1, 2, 3):
        remote(
            u_part.at[pl.ds(0, 2)],
            u_in_x.at[dx - 1],
            x_send.at[dx - 1],
            x_recv.at[dx - 1],
            (me, seat),
        ).wait_recv()
    for which in range(2):
        u_mid[which] = (
            u_part[x * 2 + which].astype(F32)
            + u_in_x[0, which].astype(F32)
            + u_in_x[1, which].astype(F32)
            + u_in_x[2, which].astype(F32)
        ).astype(BF16)
    fold = []
    for which in range(2):
        target = slot * 8 + x * 2 + which
        itself = jnp.logical_and(plane == me, target == seat)
        copy = remote(
            u_mid.at[which],
            u_in_z.at[half],
            z_send.at[which],
            z_recv.at[half],
            (plane, target),
        )
        fold.append((itself, copy))

        @pl.when(jnp.logical_not(itself))
        def _():
            copy.start()

        @pl.when(itself)
        def _():
            u_in_z[half] = u_mid[which]

    for step in range(1, 8):
        remote(
            table_out.at[0],
            table_in.at[step - 1],
            t_send.at[step - 1],
            t_recv.at[step - 1],
            (me, seat),
        ).wait_recv()
    folded = table_out[me]
    for step in range(1, 8):
        folded = folded + table_in[step - 1]
    table[...] = folded
    diagonal = lax.div(iota((VAR_CHUNK, CHUNK), 1), PIX) == iota((VAR_CHUNK, CHUNK), 0)
    for chunk in range(ROWS // CHUNK):
        span = slice(chunk * CHUNK, chunk * CHUNK + CHUNK)
        block = jnp.concatenate(
            [
                jnp.where(diagonal, table[head : head + 1, span], 0.0)
                for head in range(HEADS_DEV)
            ],
            axis=0,
        )
        high = block.astype(BF16)
        low = (block - high.astype(F32)).astype(BF16)
        pair = jnp.dot(
            jnp.concatenate([high, low], axis=0), patches[span], preferred_element_type=F32
        )
        pair = pair[0:64] + pair[64:128]
        pick = iota((VAR_CHUNK, 128), 1) == iota((VAR_CHUNK, 128), 0) + chunk * VAR_CHUNK
        for head in range(HEADS_DEV):
            base = jnp.sum(
                jnp.where(pick, table[head : head + 1, ROWS:DEPTH], 0.0), axis=1, keepdims=True
            )
            scores[head, chunk * VAR_CHUNK : (chunk + 1) * VAR_CHUNK] = (
                pair[head * VAR_CHUNK : (head + 1) * VAR_CHUNK] + base
            )
    for head in range(HEADS_DEV):
        raised = jnp.exp(scores[head]) * mask[...]
        attention[head] = (raised / jnp.sum(raised, axis=0, keepdims=True)).astype(BF16)

    for source in range(2):
        away = jnp.logical_or(y * 2 + source != me, me * 4 + zlo != seat)

        @pl.when(away)
        def _():
            remote(
                u_mid.at[0],
                u_in_z.at[source],
                z_send.at[0],
                z_recv.at[source],
                (me, seat),
            ).wait_recv()

    u_all[seat] = (u_in_z[0].astype(F32) + u_in_z[1].astype(F32)).astype(BF16)
    u_gather.own()
    o_gather.line()

    spread = (lax.div(iota((CHUNK, VAR_CHUNK), 0), PIX) == iota((CHUNK, VAR_CHUNK), 1)).astype(
        BF16
    )
    for head in range(HEADS_DEV):
        for chunk in range(ROWS // CHUNK):
            span = slice(chunk * CHUNK, chunk * CHUNK + CHUNK)
            wide = jnp.dot(
                spread,
                attention[head, chunk * VAR_CHUNK : (chunk + 1) * VAR_CHUNK],
                preferred_element_type=F32,
            )
            weighted[head, span] = wide.astype(BF16) * patches[span]
        weighted[head, ROWS : ROWS + VARS] = attention[head]
        weighted[head, ROWS + VARS :] = jnp.zeros((DEPTH - ROWS - VARS, TOK), BF16)

    u_gather.line()
    u_gather.ring()
    u_gather.far()
    o_gather.ring()
    u_gather.sibling()

    for head in range(HEADS_DEV):
        columns = jnp.dot(
            u_all[head * 8 : head * 8 + 8].reshape(128, DEPTH),
            weighted[head],
            preferred_element_type=F32,
        )
        heads[me, :, head * 128 : head * 128 + 128] = columns.T.astype(BF16)

    right, left = lax.rem(x + 1, 4), lax.rem(x + 3, 4)
    across = lax.rem(x + 2, 4)
    other = 1 - half
    p_count = [0]

    def send_heads(src, target):
        go(
            src,
            src,
            p_send.at[p_count[0]],
            p_recv.at[p_count[0]],
            (target, seat),
        )
        p_count[0] += 1

    def heads_here(ref, index):
        remote(ref, ref, p_send.at[index], p_recv.at[index], (me, seat)).wait_recv()

    send_heads(heads.at[me], x * 2 + other)
    send_heads(heads.at[me], right * 2 + half)
    send_heads(heads.at[me], left * 2 + half)

    o_gather.far()
    o_gather.sibling()
    total[...] = jnp.broadcast_to(bias[...].astype(F32), total.shape)

    def add(block):
        for quarter in range(4):
            span = slice(quarter * 128, quarter * 128 + 128)
            total[:, span] += jnp.dot(
                heads[block], o_all[block * 4 + quarter], preferred_element_type=F32
            )

    low_rows, high_rows = pl.ds(0, 128), pl.ds(128, 128)
    add(me)
    partner = x * 2 + other
    heads_here(heads.at[partner], 0)
    send_heads(heads.at[partner], right * 2 + half)
    send_heads(heads.at[partner], left * 2 + half)
    add(partner)
    for turn in range(2):
        which = half if turn == 0 else other
        heads_here(heads.at[left * 2 + which], 1 + 2 * turn)
        send_heads(heads.at[left * 2 + which, low_rows], right * 2 + half)
        heads_here(heads.at[right * 2 + which], 2 + 2 * turn)
        send_heads(heads.at[right * 2 + which, high_rows], left * 2 + half)
        add(left * 2 + which)
        add(right * 2 + which)
    for turn in range(2):
        which = half if turn == 0 else other
        heads_here(heads.at[across * 2 + which, low_rows], 5 + 2 * turn)
        heads_here(heads.at[across * 2 + which, high_rows], 6 + 2 * turn)
        add(across * 2 + which)
    out[...] = total[...].astype(BF16)

    for copy in sent:
        copy.wait_send()

    @pl.when(jnp.logical_not(stays))
    def _():
        swap.wait_send()

    for itself, copy in fold:

        @pl.when(jnp.logical_not(itself))
        def _():
            copy.wait_send()


def local(
    patches, embed_weight, var_embed, key_query, var_mask, value_weight, out_weight, out_bias
):
    left_side = jnp.concatenate([value_weight[:, 0, :].T, key_query.T], axis=0)
    vmem = pl.BlockSpec(memory_space=pltpu.VMEM)
    sems = pltpu.SemaphoreType.DMA
    return pl.pallas_call(
        kernel,
        out_shape=jax.ShapeDtypeStruct((TOK, COLS), BF16),
        in_specs=[vmem] * 7,
        out_specs=vmem,
        scratch_shapes=[
            pltpu.VMEM((32, COLS, 128), BF16),
            pltpu.VMEM((32, 16, DEPTH), BF16),
            pltpu.VMEM((8, 4, DEPTH), F32),
            pltpu.VMEM((7, 4, DEPTH), F32),
            pltpu.VMEM((8, 16, DEPTH), BF16),
            pltpu.VMEM((3, 2, 16, DEPTH), BF16),
            pltpu.VMEM((2, 16, DEPTH), BF16),
            pltpu.VMEM((2, 16, DEPTH), BF16),
            pltpu.VMEM((128, COLS), BF16),
            pltpu.VMEM((4, DEPTH), F32),
            pltpu.VMEM((HEADS_DEV, VARS, TOK), F32),
            pltpu.VMEM((HEADS_DEV, VARS, TOK), BF16),
            pltpu.VMEM((HEADS_DEV, DEPTH, TOK), BF16),
            pltpu.VMEM((8, TOK, COLS), BF16),
            pltpu.VMEM((TOK, COLS), F32),
            sems((31 + 3,)),
            sems((32,)),
            sems((31 + 3,)),
            sems((32,)),
            sems((2,)),
            sems((7,)),
            sems((7,)),
            sems((3,)),
            sems((3,)),
            sems((2,)),
            sems((2,)),
            sems((9,)),
            sems((9,)),
        ],
        compiler_params=pltpu.CompilerParams(
            has_side_effects=True, vmem_limit_bytes=48 * 1024 * 1024
        ),
        cost_estimate=pl.CostEstimate(
            flops=2_000_000_000, bytes_accessed=4_000_000, transcendentals=100_000
        ),
        name="aggregate",
    )(
        patches.reshape(ROWS, TOK),
        embed_weight.reshape(ROWS, COLS),
        var_embed,
        left_side,
        var_mask.astype(F32).reshape(VARS, 1),
        out_weight,
        out_bias.reshape(1, COLS),
    )


def solution(mesh):
    placed = (
        P(None, None, "seq"),
        P(None, None, "var"),
        P(None, "var"),
        P("var", None),
        P(),
        P("var", "seq", None),
        P("var", "seq"),
        P("var"),
    )
    return jax.shard_map(
        local, mesh=mesh, in_specs=placed, out_specs=P("seq", "var"), check_vma=False
    )
```

time: 573 us -> 113 us (0.20)
  waiting for transfers between devices: 470 us -> 0 us
  Pallas kernels: 0 us -> 103 us
  matrix products: 76.2 us -> 0 us
  between operations: 14.6 us -> 0.03 us
    psum x1 -> x0, waiting for transfers between devices: 288 us -> none  [local(): scores = lax.psum(partial_scores, 'var')]
    reduce_scatter x2 -> x0, waiting for transfers between devices: 138 us -> none  [the longest x1 91 us: local(): lax.psum_scatter(partial_out.astype(jnp.bfloat16), 'var', scatter_dimensi...]
    pallas_call x0 -> x1, Pallas kernels: none -> 103 us  [local(): pl.pallas_call(kernel, out_shape=jax.ShapeDtypeStruct((TOK, COLS), BF16),...]
    dot_general x5 -> x0, matrix products: 76.2 us -> none  [the longest x1 29.9 us: local(): jnp.einsum('hvt,vtd->htd', attention, embedded, preferred_element_type=jn...]
    all_gather x2 -> x0, waiting for transfers between devices: 43.9 us -> none  [the longest x1 43.9 us: local(): lax.all_gather(out_weight, 'seq', axis=1, tiled=True)]
  transfers between devices with their start and end apart: 5 -> 0, of which waited for: 4 -> 0; matrix products, arithmetic and copies ran while one was open for 8% -> 0% of each run, Pallas kernels for 0% -> 0%
where the time goes in v2:
time: 113 us; the launch traced here: 112 us
  Pallas kernels  103 us (91%)
  local copies, waits for them, and re-layouts  6.83 us (6%)
  other arithmetic  1.43 us (1%)
    pallas_call x1, Pallas kernels, local(): pl.pallas_call(kernel, out_shape=jax.ShapeDtypeStruct((TOK, COLS), BF16),...  103 us
    unnamed x10, local copies, waits for them, and re-layouts  6.04 us

profile of v2, /device:TPU:1, one launch (start us, length us, event | category | flops | bytes accessed | tf_op | source)
XLA Modules:
  0.0 111.6 jit_solution(129769384552919459)
XLA Ops:
  0.0 0.7 convert_bitcast_fusion
  0.7 0.7 reshape.15.bias
  1.3 0.1 copy.10.mask
  1.4 1.0 copy.9
  2.5 0.8 pad_maximum_fusion.left_side
  3.2 0.0 copy-start
  3.2 1.4 %copy-done = bf16[96,16,512]{2,1,0:T(8,128)(2,1)S(1)} copy-done((bf16[96,16,512]{2,1,0:T(8,128)(2,1)S(1)}, bf16[96,16,512]{2,1,0:T(8,128)(2,1)}, u32[]{:S(2)}) %copy-start) | copy-done | bytes 1572888
  4.6 0.0 copy-start.1
  4.6 1.1 %copy-done.1 = bf16[96,16,256]{2,1,0:T(8,128)(2,1)S(1)} copy-done((bf16[96,16,256]{2,1,0:T(8,128)(2,1)S(1)}, bf16[96,16,256]{2,1,0:T(8,128)(2,1)}, u32[]{:S(2)}) %copy-start.1) | copy-done | bytes 786456
  5.8 0.0 copy-start.2
  5.8 0.9 copy-done.2
  6.7 0.0 copy-start.3
  6.7 0.9 copy-done.3
  7.6 103.3 %aggregate.1 = bf16[256,512]{1,0:T(8,128)(2,1)S(1)} custom-call(bf16[1536,256]{1,0:T(8,128)(2,1)S(1)} %bitcast.9, bf16[1536,512]{1,0:T(8,128)(2,1)S(1)} %bitcast.8, bf16[96,512]{1,0:T(8,128)(2,1)S(1)} %copy-done.3, bf16[160,512]{1,0:T(8,128)(2,1)S(1)} %pad_maximum_fusion.left_side, f32[96,1]{1,0:T(8,128)S(1)} %copy.10.mask, bf16[512,128]{1,0:T(8,128)(2,1)S(1)} %copy-done.2, ...), custom_call_target="tpu_custom_call" | custom-call | flops 2000000000 | bytes 4000000 | tf_op jit(solution)/shard_map/aggregate/pallas_call | solution.py:409
  110.9 0.7 copy.12
Async XLA Ops:
  3.2 1.4 %copy-start = (bf16[96,16,512]{2,1,0:T(8,128)(2,1)S(1)}, bf16[96,16,512]{2,1,0:T(8,128)(2,1)}, u32[]{:S(2)}) copy-start(bf16[96,16,512]{2,1,0:T(8,128)(2,1)} %param.9) | copy-start | bytes 4718596
  4.6 1.1 %copy-start.1 = (bf16[96,16,256]{2,1,0:T(8,128)(2,1)S(1)}, bf16[96,16,256]{2,1,0:T(8,128)(2,1)}, u32[]{:S(2)}) copy-start(bf16[96,16,256]{2,1,0:T(8,128)(2,1)} %param.8) | copy-start | bytes 2359300
  5.8 0.9 copy-start.2
  6.7 0.9 copy-start.3

commit v3 on v2

v3 whole, which is shorter than its diff:
```python
import jax
import jax.numpy as jnp
from jax import lax
from jax.experimental import pallas as pl
from jax.experimental.pallas import tpu as pltpu
from jax.sharding import PartitionSpec as P

MESH = pl.DeviceIdType.MESH
F32 = jnp.float32
BF16 = jnp.bfloat16
VARS, PIX, TOK = 96, 16, 256
ROWS = VARS * PIX
DEPTH = ROWS + 128
CHUNK = 256
VAR_CHUNK = CHUNK // PIX
HEADS_DEV = 8
COLS = 512


def iota(shape, dim):
    return lax.broadcasted_iota(jnp.int32, shape, dim)


def kernel(
    patches_hbm,
    weight_hbm,
    embed_hbm,
    query_hbm,
    value_hbm,
    out_weight,
    mask,
    bias,
    out,
    patches,
    weight,
    embed_pad,
    value,
    left_side,
    o_all,
    u_all,
    table_out,
    table_in,
    table_mid,
    table_far,
    table,
    u_part,
    u_in_x,
    u_mid,
    u_in_z,
    scores,
    attention,
    weighted,
    heads,
    part_out,
    part_in,
    total,
    l_sem,
    o_send,
    o_recv,
    u_send,
    u_recv,
    o_swap,
    t_send,
    t_recv,
    x_send,
    x_recv,
    z_send,
    z_recv,
    p_send,
    p_recv,
):
    me = lax.axis_index("var")
    seat = lax.axis_index("seq")
    x, half = lax.div(me, 2), lax.rem(me, 2)
    zlo, y, core = lax.div(seat, 8), lax.rem(lax.div(seat, 2), 4), lax.rem(seat, 2)
    lane = lax.rem(seat, 8)
    z = half * 4 + zlo

    def turned(dz, dy, dc=0):
        return (
            lax.rem(z + dz + 8, 8),
            lax.rem(y + dy + 4, 4),
            lax.rem(core + dc, 2),
        )

    def device(z2, y2, c2):
        return (x * 2 + lax.div(z2, 4), lax.rem(z2, 4) * 8 + y2 * 2 + c2)

    loads = [
        pltpu.make_async_copy(value_hbm, value, l_sem.at[0]),
        pltpu.make_async_copy(query_hbm, left_side.at[pl.ds(128, 32)], l_sem.at[1]),
        pltpu.make_async_copy(embed_hbm, embed_pad.at[pl.ds(0, VARS)], l_sem.at[2]),
    ]
    for part in range(3):
        span = pl.ds(part * 512, 512)
        loads.append(
            pltpu.make_async_copy(weight_hbm.at[span], weight.at[span], l_sem.at[3 + part])
        )
    loads.append(pltpu.make_async_copy(patches_hbm, patches, l_sem.at[6]))

    swaps = lax.div(y, 2) != half
    swap_to = (x * 2 + 1 - half, (3 - zlo) * 8 + lax.rem(y + 2, 4) * 2 + core)
    fold_seat = x * 8 + lane
    here = [
        jnp.logical_and(zlo * 2 + which == me, fold_seat == seat) for which in range(2)
    ]
    barrier = pltpu.get_barrier_semaphore()

    def greet(target):
        pl.semaphore_signal(barrier, inc=1, device_id=target, device_id_type=MESH)

    for dx in (1, 2, 3):
        greet((lax.rem(x + dx, 4) * 2 + half, seat))
    for dz in (4, 3, -3, 2, -2, 1, -1):
        greet(device(*turned(dz, 0)))
    for dy in (1, -1):
        greet(device(*turned(0, dy)))
    greet(device(*turned(0, 0, 1)))
    for which in range(2):

        @pl.when(jnp.logical_not(here[which]))
        def _():
            greet((zlo * 2 + which, fold_seat))

    @pl.when(swaps)
    def _():
        greet(swap_to)

    for copy in loads:
        copy.start()
    stay = pltpu.make_async_copy(out_weight, o_all.at[seat], l_sem.at[7])

    @pl.when(jnp.logical_not(swaps))
    def _():
        stay.start()

    def remote(src, dst, send, recv, target):
        return pltpu.make_async_remote_copy(
            src_ref=src,
            dst_ref=dst,
            send_sem=send,
            recv_sem=recv,
            device_id=target,
            device_id_type=MESH,
        )

    sent = []

    def go(*args):
        copy = remote(*args)
        copy.start()
        sent.append(copy)

    class Gather:
        def __init__(self, buf, send, recv, index, steps):
            self.buf, self.send, self.recv, self.count = buf, send, recv, 0
            self.index, self.steps = index, steps

        def push(self, spot, target):
            piece = self.index(*spot)
            go(
                self.buf.at[piece],
                self.buf.at[piece],
                self.send.at[self.count],
                self.recv.at[piece],
                device(*target),
            )
            self.count += 1

        def arrive(self, spot):
            piece = self.index(*spot)
            remote(
                self.buf.at[piece],
                self.buf.at[piece],
                self.send.at[0],
                self.recv.at[piece],
                (me, seat),
            ).wait_recv()

        def own(self):
            spot = turned(0, 0)
            for step in self.steps:
                self.push(spot, self.along(step))
            self.sides(spot)

        def along(self, step, dy=0, dc=0):
            spot = turned(step, dy, dc)
            if self.steps == (1, 2, 3):
                spot = (half * 4 + lax.rem(zlo + step + 4, 4),) + spot[1:]
            return spot

        def sides(self, spot):
            self.push(spot, turned(0, 1))
            self.push(spot, turned(0, -1))
            self.push(spot, turned(0, 0, 1))

        def line(self):
            for step in self.steps:
                spot = self.along(-step)
                self.arrive(spot)
                self.sides(spot)

        def ring_one(self, place):
            step = ((0,) + self.steps)[place]
            left, right = self.along(-step, -1), self.along(-step, 1)
            self.arrive(left)
            if place % 2 == 0:
                self.push(left, turned(0, 1))
            self.push(left, turned(0, 0, 1))
            self.arrive(right)
            if place % 2 == 1:
                self.push(right, turned(0, -1))
            self.push(right, turned(0, 0, 1))

        def ring(self):
            for place in range(len(self.steps) + 1):
                self.ring_one(place)

        def far(self):
            for step in (0,) + self.steps:
                spot = self.along(-step, 2)
                self.arrive(spot)
                self.push(spot, turned(0, 0, 1))

        def sibling(self, dy):
            for step in (0,) + self.steps:
                self.arrive(self.along(-step, dy, 1))

    o_gather = Gather(
        o_all,
        o_send,
        o_recv,
        lambda z2, y2, c2: lax.rem(z2, 4) * 8 + y2 * 2 + c2,
        (1, 2, 3),
    )
    u_gather = Gather(
        u_all,
        u_send,
        u_recv,
        lambda z2, y2, c2: (y2 * 2 + c2) * 8 + lax.rem(z2, 4) * 2 + lax.div(z2, 4),
        (1, -1, 2, -2, 3, -3, 4),
    )
    swap = remote(
        out_weight,
        o_all.at[(3 - zlo) * 8 + lax.rem(y + 2, 4) * 2 + core],
        o_swap.at[0],
        o_swap.at[1],
        swap_to,
    )

    embed_pad[VARS:] = jnp.zeros((128 - VARS, COLS), BF16)
    for copy in loads[:3]:
        copy.wait()
    left_side[0:128] = value[...].astype(F32).T.astype(BF16)
    for part in (3, 0, 1, 2):
        wide = 512 if part < 3 else 128
        if part < 3:
            loads[3 + part].wait()
            rhs = weight[part * 512 : part * 512 + 512]
        else:
            rhs = embed_pad[...]
        both = lax.dot_general(
            left_side[...], rhs, (((1,), (1,)), ((), ())), preferred_element_type=F32
        )
        for group in range(8):
            u_part[group, :, part * 512 : part * 512 + wide] = both[
                group * 16 : group * 16 + 16
            ].astype(BF16)
        for group in range(4):
            table_out[group, :, part * 512 : part * 512 + wide] = both[
                128 + group * 8 : 136 + group * 8
            ]

    pl.semaphore_wait(
        barrier, 15 - here[0].astype(jnp.int32) - here[1].astype(jnp.int32) + swaps.astype(jnp.int32)
    )

    for dx in (2, 1, 3):
        target = lax.rem(x + dx, 4)
        go(
            u_part.at[pl.ds(target * 2, 2)],
            u_in_x.at[dx - 1],
            x_send.at[dx - 1],
            x_recv.at[dx - 1],
            (target * 2 + half, seat),
        )

    @pl.when(swaps)
    def _():
        swap.start()

    for dx in (2, 1, 3):
        target = lax.rem(x + dx, 4)
        go(
            table_out.at[target],
            table_in.at[dx - 1],
            t_send.at[dx - 1],
            t_recv.at[dx - 1],
            (target * 2 + half, seat),
        )

    def landed(ref, send, recv):
        remote(ref, ref, send, recv, (me, seat)).wait_recv()

    for dx in (1, 3, 2):
        landed(u_in_x.at[dx - 1], x_send.at[0], x_recv.at[dx - 1])
    for which in range(2):
        u_mid[which] = (
            u_part[x * 2 + which].astype(F32)
            + u_in_x[0, which].astype(F32)
            + u_in_x[1, which].astype(F32)
            + u_in_x[2, which].astype(F32)
        ).astype(BF16)
    fold = []
    for which in range(2):
        copy = remote(
            u_mid.at[which],
            u_in_z.at[half],
            z_send.at[which],
            z_recv.at[half],
            (zlo * 2 + which, fold_seat),
        )
        fold.append(copy)

        @pl.when(jnp.logical_not(here[which]))
        def _():
            copy.start()

        @pl.when(here[which])
        def _():
            u_in_z[half] = u_mid[which]

    for dx in (1, 3, 2):
        landed(table_in.at[dx - 1], t_send.at[0], t_recv.at[dx - 1])
    table_mid[...] = table_out[x] + table_in[0] + table_in[1] + table_in[2]
    go(
        table_mid,
        table_far,
        t_send.at[3],
        t_recv.at[3],
        (x * 2 + 1 - half, seat),
    )

    @pl.when(swaps)
    def _():
        landed(o_all.at[seat], o_swap.at[0], o_swap.at[1])

    @pl.when(jnp.logical_not(swaps))
    def _():
        stay.wait()

    o_gather.own()

    loads[6].wait()
    landed(table_far, t_send.at[0], t_recv.at[3])
    table[...] = table_mid[...] + table_far[...]
    diagonal = lax.div(iota((VAR_CHUNK, CHUNK), 1), PIX) == iota((VAR_CHUNK, CHUNK), 0)
    stacked = HEADS_DEV * VAR_CHUNK
    for chunk in range(ROWS // CHUNK):
        span = slice(chunk * CHUNK, chunk * CHUNK + CHUNK)
        block = jnp.concatenate(
            [
                jnp.where(diagonal, table[head : head + 1, span], 0.0)
                for head in range(HEADS_DEV)
            ],
            axis=0,
        )
        high = block.astype(BF16)
        low = (block - high.astype(F32)).astype(BF16)
        pair = jnp.dot(
            jnp.concatenate([high, low], axis=0), patches[span], preferred_element_type=F32
        )
        pair = pair[0:stacked] + pair[stacked : 2 * stacked]
        pick = iota((VAR_CHUNK, 128), 1) == iota((VAR_CHUNK, 128), 0) + chunk * VAR_CHUNK
        for head in range(HEADS_DEV):
            base = jnp.sum(
                jnp.where(pick, table[head : head + 1, ROWS:DEPTH], 0.0), axis=1, keepdims=True
            )
            scores[head, chunk * VAR_CHUNK : (chunk + 1) * VAR_CHUNK] = (
                pair[head * VAR_CHUNK : (head + 1) * VAR_CHUNK] + base
            )
    spread = (lax.div(iota((CHUNK, VAR_CHUNK), 0), PIX) == iota((CHUNK, VAR_CHUNK), 1)).astype(
        BF16
    )

    def weigh(head):
        raised = jnp.exp(scores[head]) * mask[...]
        attention[head] = (raised / jnp.sum(raised, axis=0, keepdims=True)).astype(BF16)
        for chunk in range(ROWS // CHUNK):
            span = slice(chunk * CHUNK, chunk * CHUNK + CHUNK)
            wide = jnp.dot(
                spread,
                attention[head, chunk * VAR_CHUNK : (chunk + 1) * VAR_CHUNK],
                preferred_element_type=F32,
            )
            weighted[head, span] = wide.astype(BF16) * patches[span]
        weighted[head, ROWS : ROWS + VARS] = attention[head]
        weighted[head, ROWS + VARS :] = jnp.zeros((DEPTH - ROWS - VARS, TOK), BF16)

    for head in range(HEADS_DEV):
        weigh(head)

    for source in range(2):

        @pl.when(jnp.logical_not(here[source]))
        def _():
            landed(u_in_z.at[source], z_send.at[0], z_recv.at[source])

    u_all[lane * 8 + zlo * 2 + half] = (u_in_z[0].astype(F32) + u_in_z[1].astype(F32)).astype(
        BF16
    )
    u_gather.own()
    o_gather.line()
    u_gather.line()

    def project(dy, dc):
        head = lax.rem(y + dy + 4, 4) * 2 + lax.rem(core + dc, 2)
        columns = jnp.dot(
            u_all[pl.ds(head * 8, 8)].reshape(128, DEPTH),
            weighted[head],
            preferred_element_type=F32,
        )
        heads[:, pl.ds(pl.multiple_of(head * 128, 128), 128)] = columns.T.astype(BF16)

    project(0, 0)
    u_gather.ring()
    o_gather.ring()
    project(-1, 0)
    project(1, 0)
    u_gather.far()
    project(2, 0)
    for dy in (0, -1, 1, 2):
        u_gather.sibling(dy)
        project(dy, 1)
    o_gather.far()
    for dy in (0, -1, 1, 2):
        o_gather.sibling(dy)

    def partial(target, dst):
        near = target * 8 + half * 4
        far = (3 - target) * 8 + (1 - half) * 4
        for quarter in range(4):
            own_rows = jnp.dot(
                heads[:, pl.ds(pl.multiple_of(half * 512, 512), 512)],
                o_all[near + quarter],
                preferred_element_type=F32,
            )
            other_rows = jnp.dot(
                heads[:, pl.ds(pl.multiple_of(512 - half * 512, 512), 512)],
                o_all[far + quarter],
                preferred_element_type=F32,
            )
            dst[:, quarter * 128 : quarter * 128 + 128] = (own_rows + other_rows).astype(
                dst.dtype
            )

    for dx in (2, 1, 3):
        target = lax.rem(x + dx, 4)
        partial(target, part_out.at[dx - 1])
        go(
            part_out.at[dx - 1],
            part_in.at[dx - 1],
            p_send.at[dx - 1],
            p_recv.at[dx - 1],
            (target * 2 + half, seat),
        )
    partial(x, total)
    for dx in (1, 3, 2):
        landed(part_in.at[dx - 1], p_send.at[0], p_recv.at[dx - 1])
    out[...] = (
        total[...]
        + part_in[0].astype(F32)
        + part_in[1].astype(F32)
        + part_in[2].astype(F32)
        + bias[...].astype(F32)
    ).astype(BF16)

    for copy in sent:
        copy.wait_send()

    @pl.when(swaps)
    def _():
        swap.wait_send()

    for which in range(2):

        @pl.when(jnp.logical_not(here[which]))
        def _():
            fold[which].wait_send()


def local(
    patches, embed_weight, var_embed, key_query, var_mask, value_weight, out_weight, out_bias
):
    vmem = pl.BlockSpec(memory_space=pltpu.VMEM)
    hbm = pl.BlockSpec(memory_space=pl.ANY)
    sems = pltpu.SemaphoreType.DMA
    return pl.pallas_call(
        kernel,
        out_shape=jax.ShapeDtypeStruct((TOK, COLS), BF16),
        in_specs=[hbm] * 6 + [vmem] * 2,
        out_specs=vmem,
        scratch_shapes=[
            pltpu.VMEM((ROWS, TOK), BF16),
            pltpu.VMEM((ROWS, COLS), BF16),
            pltpu.VMEM((128, COLS), BF16),
            pltpu.VMEM((COLS, 128), BF16),
            pltpu.VMEM((160, COLS), BF16),
            pltpu.VMEM((32, COLS, 128), BF16),
            pltpu.VMEM((64, 16, DEPTH), BF16),
            pltpu.VMEM((4, 8, DEPTH), F32),
            pltpu.VMEM((3, 8, DEPTH), F32),
            pltpu.VMEM((8, DEPTH), F32),
            pltpu.VMEM((8, DEPTH), F32),
            pltpu.VMEM((8, DEPTH), F32),
            pltpu.VMEM((8, 16, DEPTH), BF16),
            pltpu.VMEM((3, 2, 16, DEPTH), BF16),
            pltpu.VMEM((2, 16, DEPTH), BF16),
            pltpu.VMEM((2, 16, DEPTH), BF16),
            pltpu.VMEM((HEADS_DEV, VARS, TOK), F32),
            pltpu.VMEM((HEADS_DEV, VARS, TOK), BF16),
            pltpu.VMEM((HEADS_DEV, DEPTH, TOK), BF16),
            pltpu.VMEM((TOK, 1024), BF16),
            pltpu.VMEM((3, TOK, COLS), BF16),
            pltpu.VMEM((3, TOK, COLS), BF16),
            pltpu.VMEM((TOK, COLS), F32),
            sems((8,)),
            sems((31,)),
            sems((32,)),
            sems((63,)),
            sems((64,)),
            sems((2,)),
            sems((4,)),
            sems((4,)),
            sems((3,)),
            sems((3,)),
            sems((2,)),
            sems((2,)),
            sems((3,)),
            sems((3,)),
        ],
        compiler_params=pltpu.CompilerParams(
            has_side_effects=True, collective_id=0, vmem_limit_bytes=56 * 1024 * 1024
        ),
        cost_estimate=pl.CostEstimate(
            flops=2_000_000_000, bytes_accessed=4_000_000, transcendentals=200_000
        ),
        name="aggregate",
    )(
        patches.reshape(ROWS, TOK),
        embed_weight.reshape(ROWS, COLS),
        var_embed,
        key_query.T,
        value_weight.reshape(COLS, 128),
        out_weight,
        var_mask.astype(F32).reshape(VARS, 1),
        out_bias.reshape(1, COLS),
    )


def solution(mesh):
    placed = (
        P(None, None, "seq"),
        P(None, None, "var"),
        P(None, "var"),
        P("var", None),
        P(),
        P("var", "seq", None),
        P("var", "seq"),
        P("var"),
    )
    return jax.shard_map(
        local, mesh=mesh, in_specs=placed, out_specs=P("seq", "var"), check_vma=False
    )
```

time: 113 us -> 85.2 us (0.75)
  Pallas kernels: 103 us -> 80.3 us
  local copies, waits for them, and re-layouts: 6.83 us -> 3.64 us
    pallas_call x1, Pallas kernels: 103 us -> 80.3 us  [local(): pl.pallas_call(kernel, out_shape=jax.ShapeDtypeStruct((TOK, COLS), BF16),...]
    unnamed x10 -> x1, local copies, waits for them, and re-layouts: 6.04 us -> 1.67 us
where the time goes in v3:
time: 85.2 us; the launch traced here: 84.6 us
  Pallas kernels  80.3 us (94%)
  local copies, waits for them, and re-layouts  3.64 us (4%)
    pallas_call x1, Pallas kernels, local(): pl.pallas_call(kernel, out_shape=jax.ShapeDtypeStruct((TOK, COLS), BF16),...  80.3 us

profile of v3, /device:TPU:1, one launch (start us, length us, event | category | flops | bytes accessed | tf_op | source)
XLA Modules:
  0.0 84.6 jit_solution(14300870063049291863)
XLA Ops:
  0.0 0.7 convert_bitcast_fusion
  0.7 1.3 %reshape.19.bias = bf16[1,512]{1,0:T(2,128)(2,1)} reshape(bf16[512]{0:T(512)(128)(2,1)} %param.15) | data formatting | bytes 2048 | tf_op jit(solution)/shard_map/reshape | solution.py:557
  1.9 0.7 copy.9.mask
  2.6 80.3 %aggregate.1 = bf16[256,512]{1,0:T(8,128)(2,1)} custom-call(bf16[1536,256]{1,0:T(8,128)(2,1)} %bitcast.7, bf16[1536,512]{1,0:T(8,128)(2,1)} %bitcast.6, bf16[96,512]{1,0:T(8,128)(2,1)} %embed_hbm.1, bf16[32,512]{1,0:T(8,128)(2,1)} %bitcast.9, bf16[512,128]{1,0:T(8,128)(2,1)} %bitcast.8, bf16[512,128]{1,0:T(8,128)(2,1)} %out_weight.1, f32[96,1]{1,0:T(8,128)} %copy.9.mask, ...), custom_call_target="tpu_custom_call" | custom-call | flops 2000000000 | bytes 4000000 | tf_op jit(solution)/shard_map/aggregate/pallas_call | solution.py:498
  82.9 1.7 %copy.11 = bf16[256,512]{1,0:T(8,128)(2,1)} copy(bf16[256,512]{1,0:T(8,128)(2,1)} %aggregate.1) | data formatting | bytes 524288

commit v4 on v3

--- a/solution.py
+++ b/solution.py
@@ -29,7 +29,6 @@
     value_hbm,
     out_weight,
     mask,
-    bias,
     out,
     patches,
     weight,
@@ -99,7 +98,7 @@
     loads.append(pltpu.make_async_copy(patches_hbm, patches, l_sem.at[6]))
 
     swaps = lax.div(y, 2) != half
-    swap_to = (x * 2 + 1 - half, (3 - zlo) * 8 + lax.rem(y + 2, 4) * 2 + core)
+    swap_to = (x * 2 + 1 - half, jnp.where(zlo < 2, 3, 0) * 8 + (3 - y) * 2 + core)
     fold_seat = x * 8 + lane
     here = [
         jnp.logical_and(zlo * 2 + which == me, fold_seat == seat) for which in range(2)
@@ -111,7 +110,7 @@
 
     for dx in (1, 2, 3):
         greet((lax.rem(x + dx, 4) * 2 + half, seat))
-    for dz in (4, 3, -3, 2, -2, 1, -1):
+    for dz in (4, 1, -1):
         greet(device(*turned(dz, 0)))
     for dy in (1, -1):
         greet(device(*turned(0, dy)))
@@ -122,9 +121,10 @@
         def _():
             greet((zlo * 2 + which, fold_seat))
 
-    @pl.when(swaps)
+    @pl.when(jnp.logical_and(swaps, lax.rem(zlo, 3) == 0))
     def _():
-        greet(swap_to)
+        for line in (3 - zlo, jnp.where(zlo == 0, 2, 1)):
+            greet((x * 2 + 1 - half, line * 8 + (3 - y) * 2 + core))
 
     for copy in loads:
         copy.start()
@@ -151,102 +151,182 @@
         copy.start()
         sent.append(copy)
 
-    class Gather:
-        def __init__(self, buf, send, recv, index, steps):
-            self.buf, self.send, self.recv, self.count = buf, send, recv, 0
-            self.index, self.steps = index, steps
+    def push(buf, piece, send, recv, target):
+        remote(buf.at[piece], buf.at[piece], send, recv.at[piece], device(*target)).start()
+
+    def arrive(buf, piece, recv):
+        remote(buf.at[piece], buf.at[piece], recv.at[piece], recv.at[piece], (me, seat)).wait_recv()
+
+    class FoldedGather:
+        steps = (1, -1, 2, -2, 3, -3, 4)
+
+        def __init__(self):
+            self.count = 0
+
+        def index(self, z2, y2, c2):
+            return (y2 * 2 + c2) * 8 + lax.rem(z2, 4) * 2 + lax.div(z2, 4)
 
         def push(self, spot, target):
-            piece = self.index(*spot)
-            go(
-                self.buf.at[piece],
-                self.buf.at[piece],
-                self.send.at[self.count],
-                self.recv.at[piece],
-                device(*target),
-            )
+            push(u_all, self.index(*spot), u_send.at[self.count], u_recv, target)
             self.count += 1
 
         def arrive(self, spot):
-            piece = self.index(*spot)
-            remote(
-                self.buf.at[piece],
-                self.buf.at[piece],
-                self.send.at[0],
-                self.recv.at[piece],
-                (me, seat),
-            ).wait_recv()
-
-        def own(self):
-            spot = turned(0, 0)
-            for step in self.steps:
-                self.push(spot, self.along(step))
-            self.sides(spot)
-
-        def along(self, step, dy=0, dc=0):
-            spot = turned(step, dy, dc)
-            if self.steps == (1, 2, 3):
-                spot = (half * 4 + lax.rem(zlo + step + 4, 4),) + spot[1:]
-            return spot
+            arrive(u_all, self.index(*spot), u_recv)
 
         def sides(self, spot):
             self.push(spot, turned(0, 1))
             self.push(spot, turned(0, -1))
             self.push(spot, turned(0, 0, 1))
 
-        def line(self):
-            for step in self.steps:
-                spot = self.along(-step)
+        def own(self):
+            for sign in (1, -1):
+                self.push(turned(0, 0), turned(sign, 0))
+            self.sides(turned(0, 0))
+
+        def line(self, distance):
+            if distance < 3:
+                for sign in (1, -1):
+                    spot = turned(-sign * distance, 0)
+                    self.arrive(spot)
+                    self.push(spot, turned(sign, 0))
+                    self.sides(spot)
+                return
+            for sign in (1, -1):
+                self.arrive(turned(-3 * sign, 0))
+            around = 1 - 2 * core
+            self.push(turned(-3 * around, 0), turned(around, 0))
+            for step in (3, -3, 4):
+                if step == 4:
+                    self.arrive(turned(4, 0))
+                self.sides(turned(step, 0))
+
+        def ring(self):
+            for place, step in enumerate((0,) + self.steps):
+                left, right = turned(-step, -1), turned(-step, 1)
+                self.arrive(left)
+                if place % 2 == 0:
+                    self.push(left, turned(0, 1))
+                self.push(left, turned(0, 0, 1))
+                self.arrive(right)
+                if place % 2 == 1:
+                    self.push(right, turned(0, -1))
+                self.push(right, turned(0, 0, 1))
+
+        def far(self):
+            for step in (0,) + self.steps:
+                self.arrive(turned(-step, 2))
+                self.push(turned(-step, 2), turned(0, 0, 1))
+
+        def sibling(self, dy):
+            for step in (0,) + self.steps:
+                self.arrive(turned(-step, dy, 1))
+
+        def finish(self):
+            for count in range(self.count):
+                landed_send(u_all.at[0], u_send.at[count])
+
+    targets = [lax.rem(x + dx, 4) for dx in (2, 1, 3, 0)]
+
+    class OutGather:
+        def __init__(self):
+            low_end = zlo < 2
+            middle = jnp.logical_and(zlo > 0, zlo < 3)
+            first, second = jnp.where(low_end, 0, 3), jnp.where(low_end, 1, 2)
+            come = (first, second, 3 - first, 3 - second)
+            twice, mirror = lax.rem(zlo + 2, 4), 3 - zlo
+            near = (
+                zlo + 1 - 2 * lax.rem(zlo, 2),
+                jnp.where(middle, mirror, twice),
+                jnp.where(middle, twice, mirror),
+                zlo,
+            )
+            self.lines = [jnp.where(swaps, a, b) for a, b in zip(come, near)]
+            self.pushed = []
+
+        def spot(self, turn, dy, dc=0):
+            y2, target = lax.rem(y + dy + 4, 4), targets[turn]
+            near = (lax.div(y2, 2) == half).astype(jnp.int32)
+            line = near * target + (1 - near) * (3 - target)
+            return half * 4 + line, y2, lax.rem(core + dc, 2)
+
+        def index(self, z2, y2, c2):
+            return lax.rem(z2, 4) * 8 + y2 * 2 + c2
+
+        def push(self, spot, target, when=None):
+            slot = len(self.pushed)
+            self.pushed.append(when)
+
+            def start():
+                push(o_all, self.index(*spot), o_send.at[slot], o_recv, target)
+
+            if when is None:
+                start()
+            else:
+                pl.when(when)(start)
+
+        def arrive(self, spot):
+            arrive(o_all, self.index(*spot), o_recv)
+
+        def sides(self, spot, when=None):
+            self.push(spot, turned(0, 1), when)
+            self.push(spot, turned(0, -1), when)
+            self.push(spot, turned(0, 0, 1), when)
+
+        def own(self):
+            mine, stays = turned(0, 0), jnp.logical_not(swaps)
+            self.push(mine, turned(1, 0), jnp.logical_and(stays, zlo < 3))
+            self.push(mine, turned(-1, 0), jnp.logical_and(stays, zlo > 0))
+            self.sides(mine, stays)
+
+        def serve(self, order):
+            line = self.lines[order]
+            spot = (half * 4 + line, y, core)
+            when = swaps if order == 3 else None
+            if when is None:
                 self.arrive(spot)
-                self.sides(spot)
-
-        def ring_one(self, place):
-            step = ((0,) + self.steps)[place]
-            left, right = self.along(-step, -1), self.along(-step, 1)
+            else:
+                pl.when(when)(lambda: self.arrive(spot))
+            up = jnp.where(swaps, line < 2, line < zlo)
+            goes = jnp.where(up, zlo < 3, zlo > 0)
+            if when is not None:
+                goes = jnp.logical_and(goes, when)
+            self.push(spot, turned(jnp.where(up, 1, -1), 0), goes)
+            self.sides(spot, when)
+
+        def ring(self, turn):
+            left, right = self.spot(turn, -1), self.spot(turn, 1)
             self.arrive(left)
-            if place % 2 == 0:
+            if turn % 2 == 0:
                 self.push(left, turned(0, 1))
             self.push(left, turned(0, 0, 1))
             self.arrive(right)
-            if place % 2 == 1:
+            if turn % 2 == 1:
                 self.push(right, turned(0, -1))
             self.push(right, turned(0, 0, 1))
 
-        def ring(self):
-            for place in range(len(self.steps) + 1):
-                self.ring_one(place)
-
-        def far(self):
-            for step in (0,) + self.steps:
-                spot = self.along(-step, 2)
-                self.arrive(spot)
-                self.push(spot, turned(0, 0, 1))
-
-        def sibling(self, dy):
-            for step in (0,) + self.steps:
-                self.arrive(self.along(-step, dy, 1))
-
-    o_gather = Gather(
-        o_all,
-        o_send,
-        o_recv,
-        lambda z2, y2, c2: lax.rem(z2, 4) * 8 + y2 * 2 + c2,
-        (1, 2, 3),
-    )
-    u_gather = Gather(
-        u_all,
-        u_send,
-        u_recv,
-        lambda z2, y2, c2: (y2 * 2 + c2) * 8 + lax.rem(z2, 4) * 2 + lax.div(z2, 4),
-        (1, -1, 2, -2, 3, -3, 4),
-    )
-    swap = remote(
-        out_weight,
-        o_all.at[(3 - zlo) * 8 + lax.rem(y + 2, 4) * 2 + core],
-        o_swap.at[0],
-        o_swap.at[1],
-        swap_to,
-    )
+        def far(self, turn):
+            spot = self.spot(turn, 2)
+            self.arrive(spot)
+            self.push(spot, turned(0, 0, 1))
+
+        def sibling(self, turn):
+            for dy in (0, -1, 1, 2):
+                self.arrive(self.spot(turn, dy, 1))
+
+        def finish(self):
+            for slot, when in enumerate(self.pushed):
+                if when is None:
+                    landed_send(o_all.at[0], o_send.at[slot])
+                else:
+                    pl.when(when)(lambda: landed_send(o_all.at[0], o_send.at[slot]))
+
+    def landed_send(ref, send):
+        remote(ref, ref, send, send, (me, seat)).wait_send()
+
+    o_gather = OutGather()
+    u_gather = FoldedGather()
+    swap_piece = (3 - zlo) * 8 + (3 - y) * 2 + core
+    swap = remote(out_weight, o_all.at[swap_piece], o_swap.at[0], o_recv.at[swap_piece], swap_to)
 
     embed_pad[VARS:] = jnp.zeros((128 - VARS, COLS), BF16)
     for copy in loads[:3]:
@@ -272,7 +352,7 @@
             ]
 
     pl.semaphore_wait(
-        barrier, 15 - here[0].astype(jnp.int32) - here[1].astype(jnp.int32) + swaps.astype(jnp.int32)
+        barrier, 11 - here[0].astype(jnp.int32) - here[1].astype(jnp.int32) + swaps.astype(jnp.int32)
     )
 
     for dx in (2, 1, 3):
@@ -289,15 +369,11 @@
     def _():
         swap.start()
 
-    for dx in (2, 1, 3):
-        target = lax.rem(x + dx, 4)
-        go(
-            table_out.at[target],
-            table_in.at[dx - 1],
-            t_send.at[dx - 1],
-            t_recv.at[dx - 1],
-            (target * 2 + half, seat),
-        )
+    @pl.when(jnp.logical_not(swaps))
+    def _():
+        stay.wait()
+
+    o_gather.own()
 
     def landed(ref, send, recv):
         remote(ref, ref, send, recv, (me, seat)).wait_recv()
@@ -330,6 +406,18 @@
         def _():
             u_in_z[half] = u_mid[which]
 
+    for dx in (2, 1, 3):
+        target = lax.rem(x + dx, 4)
+        go(
+            table_out.at[target],
+            table_in.at[dx - 1],
+            t_send.at[dx - 1],
+            t_recv.at[dx - 1],
+            (target * 2 + half, seat),
+        )
+
+    o_gather.serve(0)
+
     for dx in (1, 3, 2):
         landed(table_in.at[dx - 1], t_send.at[0], t_recv.at[dx - 1])
     table_mid[...] = table_out[x] + table_in[0] + table_in[1] + table_in[2]
@@ -341,15 +429,23 @@
         (x * 2 + 1 - half, seat),
     )
 
-    @pl.when(swaps)
-    def _():
-        landed(o_all.at[seat], o_swap.at[0], o_swap.at[1])
-
-    @pl.when(jnp.logical_not(swaps))
-    def _():
-        stay.wait()
-
-    o_gather.own()
+    for source in range(2):
+
+        @pl.when(jnp.logical_not(here[source]))
+        def _():
+            landed(u_in_z.at[source], z_send.at[0], z_recv.at[source])
+
+    u_all[lane * 8 + zlo * 2 + half] = (u_in_z[0].astype(F32) + u_in_z[1].astype(F32)).astype(
+        BF16
+    )
+    u_gather.own()
+
+    u_gather.line(1)
+    o_gather.serve(1)
+    u_gather.line(2)
+    o_gather.serve(2)
+    u_gather.line(3)
+    o_gather.serve(3)
 
     loads[6].wait()
     landed(table_far, t_send.at[0], t_recv.at[3])
@@ -383,8 +479,15 @@
         BF16
     )
 
+    flags = jnp.broadcast_to(mask[...].astype(F32).reshape(1, VARS), (VARS, VARS))
+    keep = jnp.sum(
+        jnp.where(iota((VARS, VARS), 0) == iota((VARS, VARS), 1), flags, 0.0),
+        axis=1,
+        keepdims=True,
+    )
+
     def weigh(head):
-        raised = jnp.exp(scores[head]) * mask[...]
+        raised = jnp.exp(scores[head]) * keep
         attention[head] = (raised / jnp.sum(raised, axis=0, keepdims=True)).astype(BF16)
         for chunk in range(ROWS // CHUNK):
             span = slice(chunk * CHUNK, chunk * CHUNK + CHUNK)
@@ -400,19 +503,6 @@
     for head in range(HEADS_DEV):
         weigh(head)
 
-    for source in range(2):
-
-        @pl.when(jnp.logical_not(here[source]))
-        def _():
-            landed(u_in_z.at[source], z_send.at[0], z_recv.at[source])
-
-    u_all[lane * 8 + zlo * 2 + half] = (u_in_z[0].astype(F32) + u_in_z[1].astype(F32)).astype(
-        BF16
-    )
-    u_gather.own()
-    o_gather.line()
-    u_gather.line()
-
     def project(dy, dc):
         head = lax.rem(y + dy + 4, 4) * 2 + lax.rem(core + dc, 2)
         columns = jnp.dot(
@@ -424,7 +514,8 @@
 
     project(0, 0)
     u_gather.ring()
-    o_gather.ring()
+    for turn in range(4):
+        o_gather.ring(turn)
     project(-1, 0)
     project(1, 0)
     u_gather.far()
@@ -432,13 +523,10 @@
     for dy in (0, -1, 1, 2):
         u_gather.sibling(dy)
         project(dy, 1)
-    o_gather.far()
-    for dy in (0, -1, 1, 2):
-        o_gather.sibling(dy)
 
     def partial(target, dst):
         near = target * 8 + half * 4
-        far = (3 - target) * 8 + (1 - half) * 4
+        far = (3 - target) * 8 + (1 - half) * 4 + 2
         for quarter in range(4):
             own_rows = jnp.dot(
                 heads[:, pl.ds(pl.multiple_of(half * 512, 512), 512)],
@@ -447,36 +535,52 @@
             )
             other_rows = jnp.dot(
                 heads[:, pl.ds(pl.multiple_of(512 - half * 512, 512), 512)],
-                o_all[far + quarter],
+                o_all[far + quarter - 4 * (quarter // 2)],
                 preferred_element_type=F32,
             )
             dst[:, quarter * 128 : quarter * 128 + 128] = (own_rows + other_rows).astype(
                 dst.dtype
             )
 
-    for dx in (2, 1, 3):
-        target = lax.rem(x + dx, 4)
-        partial(target, part_out.at[dx - 1])
-        go(
-            part_out.at[dx - 1],
-            part_in.at[dx - 1],
-            p_send.at[dx - 1],
-            p_recv.at[dx - 1],
-            (target * 2 + half, seat),
-        )
-    partial(x, total)
-    for dx in (1, 3, 2):
-        landed(part_in.at[dx - 1], p_send.at[0], p_recv.at[dx - 1])
-    out[...] = (
-        total[...]
-        + part_in[0].astype(F32)
-        + part_in[1].astype(F32)
-        + part_in[2].astype(F32)
-        + bias[...].astype(F32)
+    low_rows, high_rows = pl.ds(0, 128), pl.ds(128, 128)
+    right, left = (targets[1] * 2 + half, seat), (targets[2] * 2 + half, seat)
+
+    def pass_on(src, dst, slot, target):
+        go(src, dst, p_send.at[slot], p_recv.at[slot], target)
+
+    def block(turn, dst):
+        o_gather.far(turn)
+        o_gather.sibling(turn)
+        partial(targets[turn], dst)
+
+    block(0, part_out.at[0])
+    pass_on(part_out.at[0, low_rows], part_in.at[0, low_rows], 0, right)
+    pass_on(part_out.at[0, high_rows], part_in.at[0, high_rows], 1, left)
+    block(1, part_out.at[1])
+    pass_on(part_out.at[1, high_rows], part_in.at[1, high_rows], 2, right)
+    block(2, part_out.at[2])
+    pass_on(part_out.at[2, low_rows], part_in.at[2, low_rows], 3, left)
+    landed(part_in.at[0, low_rows], p_send.at[0], p_recv.at[0])
+    part_out[1, 0:128] = (
+        part_out[1, 0:128].astype(F32) + part_in[0, 0:128].astype(F32)
     ).astype(BF16)
+    pass_on(part_out.at[1, low_rows], part_in.at[1, low_rows], 4, right)
+    landed(part_in.at[0, high_rows], p_send.at[0], p_recv.at[1])
+    part_out[2, 128:256] = (
+        part_out[2, 128:256].astype(F32) + part_in[0, 128:256].astype(F32)
+    ).astype(BF16)
+    pass_on(part_out.at[2, high_rows], part_in.at[2, high_rows], 5, left)
+    block(3, total)
+    landed(part_in.at[1, high_rows], p_send.at[0], p_recv.at[2])
+    landed(part_in.at[2, low_rows], p_send.at[0], p_recv.at[3])
+    landed(part_in.at[1, low_rows], p_send.at[0], p_recv.at[4])
+    landed(part_in.at[2, high_rows], p_send.at[0], p_recv.at[5])
+    out[...] = total[...] + part_in[1].astype(F32) + part_in[2].astype(F32)
 
     for copy in sent:
         copy.wait_send()
+    o_gather.finish()
+    u_gather.finish()
 
     @pl.when(swaps)
     def _():
@@ -495,10 +599,10 @@
     vmem = pl.BlockSpec(memory_space=pltpu.VMEM)
     hbm = pl.BlockSpec(memory_space=pl.ANY)
     sems = pltpu.SemaphoreType.DMA
-    return pl.pallas_call(
+    summed = pl.pallas_call(
         kernel,
-        out_shape=jax.ShapeDtypeStruct((TOK, COLS), BF16),
-        in_specs=[hbm] * 6 + [vmem] * 2,
+        out_shape=jax.ShapeDtypeStruct((TOK, COLS), F32),
+        in_specs=[hbm] * 6 + [vmem],
         out_specs=vmem,
         scratch_shapes=[
             pltpu.VMEM((ROWS, TOK), BF16),
@@ -525,19 +629,19 @@
             pltpu.VMEM((3, TOK, COLS), BF16),
             pltpu.VMEM((TOK, COLS), F32),
             sems((8,)),
-            sems((31,)),
+            sems((41,)),
             sems((32,)),
             sems((63,)),
             sems((64,)),
-            sems((2,)),
+            sems((1,)),
             sems((4,)),
             sems((4,)),
             sems((3,)),
             sems((3,)),
             sems((2,)),
             sems((2,)),
-            sems((3,)),
-            sems((3,)),
+            sems((6,)),
+            sems((6,)),
         ],
         compiler_params=pltpu.CompilerParams(
             has_side_effects=True, collective_id=0, vmem_limit_bytes=56 * 1024 * 1024
@@ -553,9 +657,9 @@
         key_query.T,
         value_weight.reshape(COLS, 128),
         out_weight,
-        var_mask.astype(F32).reshape(VARS, 1),
-        out_bias.reshape(1, COLS),
-    )
+        var_mask,
+    )
+    return (summed + out_bias.astype(F32)[None, :]).astype(BF16)
 
 
 def solution(mesh):

time: 85.2 us -> 78.8 us (0.925)
  Pallas kernels: 80.3 us -> 76.1 us
  local copies, waits for them, and re-layouts: 3.64 us -> 0 us
  other arithmetic: 0.66 us -> 2.46 us
    pallas_call x1, Pallas kernels: 80.3 us -> 76.1 us  [local(): pl.pallas_call(kernel, out_shape=jax.ShapeDtypeStruct((TOK, COLS), F32),...]
    convert_element_type x0 -> x2, other arithmetic: none -> 2.46 us  [local(): return (summed + out_bias.astype(F32)[None, :]).astype(BF16)]
    reshape x2 -> x0, local copies, waits for them, and re-layouts: 1.97 us -> none  [the longest x1 1.25 us: local(): out_bias.reshape(1, COLS)]
    unnamed x1 -> x0, local copies, waits for them, and re-layouts: 1.67 us -> none
where the time goes in v4:
time: 78.8 us; the launch traced here: 78.6 us
  Pallas kernels  76.1 us (97%)
  other arithmetic  2.46 us (3%)
    pallas_call x1, Pallas kernels, local(): pl.pallas_call(kernel, out_shape=jax.ShapeDtypeStruct((TOK, COLS), F32),...  76.1 us
    convert_element_type x2, other arithmetic, local(): return (summed + out_bias.astype(F32)[None, :]).astype(BF16)  2.46 us

profile of v4, /device:TPU:1, one launch (start us, length us, event | category | flops | bytes accessed | tf_op | source)
XLA Modules:
  0.0 78.6 jit_solution(15817783272572141908)
XLA Ops:
  0.0 0.7 convert_element_type.6
  0.7 76.1 %aggregate.1 = f32[256,512]{1,0:T(8,128)} custom-call(bf16[1536,256]{1,0:T(8,128)(2,1)} %bitcast.5, bf16[1536,512]{1,0:T(8,128)(2,1)} %bitcast.4, bf16[96,512]{1,0:T(8,128)(2,1)} %embed_hbm.1, bf16[32,512]{1,0:T(8,128)(2,1)} %bitcast.7, bf16[512,128]{1,0:T(8,128)(2,1)} %bitcast.6, bf16[512,128]{1,0:T(8,128)(2,1)} %out_weight.1, s32[96]{0:T(128)} %mask.1), custom_call_target="tpu_custom_call" | custom-call | flops 2000000000 | bytes 4000000 | tf_op jit(solution)/shard_map/aggregate/pallas_call | solution.py:602
  76.8 1.8 %add_convert_fusion = bf16[256,512]{1,0:T(8,128)(2,1)} fusion(f32[256,512]{1,0:T(8,128)} %aggregate.1, f32[512]{0:T(512)S(1)} %convert_element_type.6), kind=kLoop, calls=%fused_computation | loop fusion | flops 262144 | bytes 788480 | tf_op jit(solution)/shard_map/convert_element_type | solution.py:662

commit v5 on v4

--- a/solution.py
+++ b/solution.py
@@ -29,6 +29,7 @@
     value_hbm,
     out_weight,
     mask,
+    bias,
     out,
     patches,
     weight,
@@ -56,13 +57,13 @@
     l_sem,
     o_send,
     o_recv,
+    o_near,
     u_send,
     u_recv,
+    u_near,
     o_swap,
-    t_send,
-    t_recv,
-    x_send,
-    x_recv,
+    t_sem,
+    x_sem,
     z_send,
     z_recv,
     p_send,
@@ -98,7 +99,7 @@
     loads.append(pltpu.make_async_copy(patches_hbm, patches, l_sem.at[6]))
 
     swaps = lax.div(y, 2) != half
-    swap_to = (x * 2 + 1 - half, jnp.where(zlo < 2, 3, 0) * 8 + (3 - y) * 2 + core)
+    swap_to = (x * 2 + 1 - half, (3 - zlo) * 8 + (3 - y) * 2 + core)
     fold_seat = x * 8 + lane
     here = [
         jnp.logical_and(zlo * 2 + which == me, fold_seat == seat) for which in range(2)
@@ -112,6 +113,8 @@
         greet((lax.rem(x + dx, 4) * 2 + half, seat))
     for dz in (4, 1, -1):
         greet(device(*turned(dz, 0)))
+    pl.when(lax.rem(zlo, 3) == 0)(lambda: greet((me, jnp.where(zlo == 0, 2, 1) * 8 + lane)))
+    pl.when(lax.rem(zlo, 3) > 0)(lambda: greet((me, lax.rem(zlo + 2, 4) * 8 + lane)))
     for dy in (1, -1):
         greet(device(*turned(0, dy)))
     greet(device(*turned(0, 0, 1)))
@@ -121,10 +124,8 @@
         def _():
             greet((zlo * 2 + which, fold_seat))
 
-    @pl.when(jnp.logical_and(swaps, lax.rem(zlo, 3) == 0))
-    def _():
-        for line in (3 - zlo, jnp.where(zlo == 0, 2, 1)):
-            greet((x * 2 + 1 - half, line * 8 + (3 - y) * 2 + core))
+    pl.when(lax.rem(zlo, 3) == 0)(lambda: greet((me, (3 - zlo) * 8 + lane)))
+    pl.when(swaps)(lambda: greet(swap_to))
 
     for copy in loads:
         copy.start()
@@ -144,39 +145,34 @@
             device_id_type=MESH,
         )
 
-    sent = []
-
-    def go(*args):
-        copy = remote(*args)
-        copy.start()
-        sent.append(copy)
-
     def push(buf, piece, send, recv, target):
-        remote(buf.at[piece], buf.at[piece], send, recv.at[piece], device(*target)).start()
-
-    def arrive(buf, piece, recv):
-        remote(buf.at[piece], buf.at[piece], recv.at[piece], recv.at[piece], (me, seat)).wait_recv()
+        remote(buf.at[piece], buf.at[piece], send, recv, device(*target)).start()
+
+    def landed(ref, recv):
+        remote(ref, ref, recv, recv, (me, seat)).wait_recv()
+
+    def left(ref, send):
+        remote(ref, ref, send, send, (me, seat)).wait_send()
 
     class FoldedGather:
         steps = (1, -1, 2, -2, 3, -3, 4)
 
-        def __init__(self):
-            self.count = 0
-
         def index(self, z2, y2, c2):
             return (y2 * 2 + c2) * 8 + lax.rem(z2, 4) * 2 + lax.div(z2, 4)
 
         def push(self, spot, target):
-            push(u_all, self.index(*spot), u_send.at[self.count], u_recv, target)
-            self.count += 1
+            push(u_all, self.index(*spot), u_send.at[0], u_recv.at[spot[1] * 8 + spot[0]], target)
 
         def arrive(self, spot):
-            arrive(u_all, self.index(*spot), u_recv)
+            landed(u_all.at[self.index(*spot)], u_recv.at[spot[1] * 8 + spot[0]])
+
+        def near(self, spot):
+            push(u_all, self.index(*spot), u_send.at[0], u_near.at[spot[1]], turned(0, 0, 1))
 
         def sides(self, spot):
             self.push(spot, turned(0, 1))
             self.push(spot, turned(0, -1))
-            self.push(spot, turned(0, 0, 1))
+            self.near(spot)
 
         def own(self):
             for sign in (1, -1):
@@ -206,42 +202,35 @@
                 self.arrive(left)
                 if place % 2 == 0:
                     self.push(left, turned(0, 1))
-                self.push(left, turned(0, 0, 1))
+                self.near(left)
                 self.arrive(right)
                 if place % 2 == 1:
                     self.push(right, turned(0, -1))
-                self.push(right, turned(0, 0, 1))
+                self.near(right)
 
         def far(self):
             for step in (0,) + self.steps:
                 self.arrive(turned(-step, 2))
-                self.push(turned(-step, 2), turned(0, 0, 1))
+                self.near(turned(-step, 2))
 
         def sibling(self, dy):
-            for step in (0,) + self.steps:
-                self.arrive(turned(-step, dy, 1))
+            y2 = lax.rem(y + dy + 4, 4)
+            landed(u_all.at[pl.ds((y2 * 2 + 1 - core) * 8, 8)], u_near.at[y2])
 
         def finish(self):
-            for count in range(self.count):
-                landed_send(u_all.at[0], u_send.at[count])
+            left(u_all.at[pl.ds(0, 63)], u_send.at[0])
 
     targets = [lax.rem(x + dx, 4) for dx in (2, 1, 3, 0)]
 
     class OutGather:
         def __init__(self):
-            low_end = zlo < 2
             middle = jnp.logical_and(zlo > 0, zlo < 3)
-            first, second = jnp.where(low_end, 0, 3), jnp.where(low_end, 1, 2)
-            come = (first, second, 3 - first, 3 - second)
             twice, mirror = lax.rem(zlo + 2, 4), 3 - zlo
-            near = (
+            self.lines = (
                 zlo + 1 - 2 * lax.rem(zlo, 2),
                 jnp.where(middle, mirror, twice),
                 jnp.where(middle, twice, mirror),
-                zlo,
             )
-            self.lines = [jnp.where(swaps, a, b) for a, b in zip(come, near)]
-            self.pushed = []
 
         def spot(self, turn, dy, dc=0):
             y2, target = lax.rem(y + dy + 4, 4), targets[turn]
@@ -252,81 +241,70 @@
         def index(self, z2, y2, c2):
             return lax.rem(z2, 4) * 8 + y2 * 2 + c2
 
-        def push(self, spot, target, when=None):
-            slot = len(self.pushed)
-            self.pushed.append(when)
-
-            def start():
-                push(o_all, self.index(*spot), o_send.at[slot], o_recv, target)
-
-            if when is None:
-                start()
-            else:
-                pl.when(when)(start)
+        def push(self, spot, target, kind):
+            recv = o_recv.at[lax.rem(spot[0], 4) * 4 + spot[1]]
+            push(o_all, self.index(*spot), o_send.at[kind], recv, target)
 
         def arrive(self, spot):
-            arrive(o_all, self.index(*spot), o_recv)
-
-        def sides(self, spot, when=None):
-            self.push(spot, turned(0, 1), when)
-            self.push(spot, turned(0, -1), when)
-            self.push(spot, turned(0, 0, 1), when)
+            landed(o_all.at[self.index(*spot)], o_recv.at[lax.rem(spot[0], 4) * 4 + spot[1]])
+
+        def near(self, spot):
+            line = lax.rem(spot[0], 4)
+            target = jnp.where(lax.div(spot[1], 2) == half, line, 3 - line)
+            push(o_all, self.index(*spot), o_send.at[0], o_near.at[target], turned(0, 0, 1))
+
+        def sides(self, spot):
+            self.push(spot, turned(0, 1), 0)
+            self.push(spot, turned(0, -1), 0)
+            self.near(spot)
 
         def own(self):
-            mine, stays = turned(0, 0), jnp.logical_not(swaps)
-            self.push(mine, turned(1, 0), jnp.logical_and(stays, zlo < 3))
-            self.push(mine, turned(-1, 0), jnp.logical_and(stays, zlo > 0))
-            self.sides(mine, stays)
-
-        def serve(self, order):
-            line = self.lines[order]
-            spot = (half * 4 + line, y, core)
-            when = swaps if order == 3 else None
-            if when is None:
+            mine = turned(0, 0)
+            for line in self.lines:
+                self.push(mine, (half * 4 + line, y, core), 1)
+            self.sides(mine)
+
+        def serve(self, order, crossed):
+            spot = (half * 4 + self.lines[order], y, core)
+
+            @pl.when(swaps if crossed else jnp.logical_not(swaps))
+            def _():
                 self.arrive(spot)
-            else:
-                pl.when(when)(lambda: self.arrive(spot))
-            up = jnp.where(swaps, line < 2, line < zlo)
-            goes = jnp.where(up, zlo < 3, zlo > 0)
-            if when is not None:
-                goes = jnp.logical_and(goes, when)
-            self.push(spot, turned(jnp.where(up, 1, -1), 0), goes)
-            self.sides(spot, when)
+                self.sides(spot)
 
         def ring(self, turn):
-            left, right = self.spot(turn, -1), self.spot(turn, 1)
-            self.arrive(left)
+            prior, following = self.spot(turn, -1), self.spot(turn, 1)
+            self.arrive(prior)
             if turn % 2 == 0:
-                self.push(left, turned(0, 1))
-            self.push(left, turned(0, 0, 1))
-            self.arrive(right)
+                self.push(prior, turned(0, 1), 0)
+            self.near(prior)
+            self.arrive(following)
             if turn % 2 == 1:
-                self.push(right, turned(0, -1))
-            self.push(right, turned(0, 0, 1))
+                self.push(following, turned(0, -1), 0)
+            self.near(following)
 
         def far(self, turn):
             spot = self.spot(turn, 2)
             self.arrive(spot)
-            self.push(spot, turned(0, 0, 1))
+            self.near(spot)
 
         def sibling(self, turn):
-            for dy in (0, -1, 1, 2):
-                self.arrive(self.spot(turn, dy, 1))
+            landed(o_all.at[pl.ds(0, 4)], o_near.at[targets[turn]])
 
         def finish(self):
-            for slot, when in enumerate(self.pushed):
-                if when is None:
-                    landed_send(o_all.at[0], o_send.at[slot])
-                else:
-                    pl.when(when)(lambda: landed_send(o_all.at[0], o_send.at[slot]))
-
-    def landed_send(ref, send):
-        remote(ref, ref, send, send, (me, seat)).wait_send()
+            left(o_all.at[pl.ds(0, 28)], o_send.at[0])
+            left(o_all.at[pl.ds(0, 3)], o_send.at[1])
 
     o_gather = OutGather()
     u_gather = FoldedGather()
     swap_piece = (3 - zlo) * 8 + (3 - y) * 2 + core
-    swap = remote(out_weight, o_all.at[swap_piece], o_swap.at[0], o_recv.at[swap_piece], swap_to)
+    swap = remote(
+        out_weight,
+        o_all.at[swap_piece],
+        o_swap.at[0],
+        o_recv.at[(3 - zlo) * 4 + 3 - y],
+        swap_to,
+    )
 
     embed_pad[VARS:] = jnp.zeros((128 - VARS, COLS), BF16)
     for copy in loads[:3]:
@@ -352,18 +330,18 @@
             ]
 
     pl.semaphore_wait(
-        barrier, 11 - here[0].astype(jnp.int32) - here[1].astype(jnp.int32) + swaps.astype(jnp.int32)
+        barrier, 12 + (lax.rem(zlo, 3) == 0).astype(jnp.int32) - here[0].astype(jnp.int32) - here[1].astype(jnp.int32) + swaps.astype(jnp.int32)
     )
 
     for dx in (2, 1, 3):
         target = lax.rem(x + dx, 4)
-        go(
+        remote(
             u_part.at[pl.ds(target * 2, 2)],
             u_in_x.at[dx - 1],
-            x_send.at[dx - 1],
-            x_recv.at[dx - 1],
+            x_sem.at[0],
+            x_sem.at[1],
             (target * 2 + half, seat),
-        )
+        ).start()
 
     @pl.when(swaps)
     def _():
@@ -372,14 +350,9 @@
     @pl.when(jnp.logical_not(swaps))
     def _():
         stay.wait()
-
-    o_gather.own()
-
-    def landed(ref, send, recv):
-        remote(ref, ref, send, recv, (me, seat)).wait_recv()
-
-    for dx in (1, 3, 2):
-        landed(u_in_x.at[dx - 1], x_send.at[0], x_recv.at[dx - 1])
+        o_gather.own()
+
+    landed(u_in_x, x_sem.at[1])
     for which in range(2):
         u_mid[which] = (
             u_part[x * 2 + which].astype(F32)
@@ -397,58 +370,71 @@
             (zlo * 2 + which, fold_seat),
         )
         fold.append(copy)
-
-        @pl.when(jnp.logical_not(here[which]))
-        def _():
-            copy.start()
+        pl.when(jnp.logical_not(here[which]))(copy.start)
 
         @pl.when(here[which])
         def _():
             u_in_z[half] = u_mid[which]
 
-    for dx in (2, 1, 3):
-        target = lax.rem(x + dx, 4)
-        go(
-            table_out.at[target],
-            table_in.at[dx - 1],
-            t_send.at[dx - 1],
-            t_recv.at[dx - 1],
-            (target * 2 + half, seat),
-        )
-
-    o_gather.serve(0)
-
-    for dx in (1, 3, 2):
-        landed(table_in.at[dx - 1], t_send.at[0], t_recv.at[dx - 1])
-    table_mid[...] = table_out[x] + table_in[0] + table_in[1] + table_in[2]
-    go(
-        table_mid,
-        table_far,
-        t_send.at[3],
-        t_recv.at[3],
-        (x * 2 + 1 - half, seat),
-    )
-
-    for source in range(2):
-
-        @pl.when(jnp.logical_not(here[source]))
-        def _():
-            landed(u_in_z.at[source], z_send.at[0], z_recv.at[source])
-
-    u_all[lane * 8 + zlo * 2 + half] = (u_in_z[0].astype(F32) + u_in_z[1].astype(F32)).astype(
-        BF16
-    )
+    def table_start():
+        for dx in (2, 1, 3):
+            target = lax.rem(x + dx, 4)
+            remote(
+                table_out.at[target],
+                table_in.at[dx - 1],
+                t_sem.at[0],
+                t_sem.at[1],
+                (target * 2 + half, seat),
+            ).start()
+
+    table_copy = remote(
+        table_mid, table_far, t_sem.at[2], t_sem.at[3], (x * 2 + 1 - half, seat)
+    )
+
+    def table_pass():
+        landed(table_in, t_sem.at[1])
+        table_mid[...] = table_out[x] + table_in[0] + table_in[1] + table_in[2]
+        table_copy.start()
+
+    def reduce_z():
+        for source in range(2):
+
+            @pl.when(jnp.logical_not(here[source]))
+            def _():
+                landed(u_in_z.at[source], z_recv.at[source])
+
+        u_all[lane * 8 + zlo * 2 + half] = (
+            u_in_z[0].astype(F32) + u_in_z[1].astype(F32)
+        ).astype(BF16)
+
+    def project(dy, dc):
+        head = lax.rem(y + dy + 4, 4) * 2 + lax.rem(core + dc, 2)
+        columns = jnp.dot(
+            u_all[pl.ds(head * 8, 8)].reshape(128, DEPTH),
+            weighted[head],
+            preferred_element_type=F32,
+        )
+        heads[:, pl.ds(pl.multiple_of(head * 128, 128), 128)] = columns.T.astype(BF16)
+
+    table_start()
+    o_gather.serve(0, 0)
+    reduce_z()
     u_gather.own()
 
+    @pl.when(swaps)
+    def _():
+        o_gather.arrive(turned(0, 0))
+        o_gather.own()
+
+    o_gather.serve(1, 0)
+    o_gather.serve(2, 0)
+    table_pass()
     u_gather.line(1)
-    o_gather.serve(1)
+    o_gather.serve(0, 1)
+    o_gather.serve(1, 1)
     u_gather.line(2)
-    o_gather.serve(2)
-    u_gather.line(3)
-    o_gather.serve(3)
-
     loads[6].wait()
-    landed(table_far, t_send.at[0], t_recv.at[3])
+    table_copy.wait_recv()
     table[...] = table_mid[...] + table_far[...]
     diagonal = lax.div(iota((VAR_CHUNK, CHUNK), 1), PIX) == iota((VAR_CHUNK, CHUNK), 0)
     stacked = HEADS_DEV * VAR_CHUNK
@@ -503,26 +489,26 @@
     for head in range(HEADS_DEV):
         weigh(head)
 
-    def project(dy, dc):
-        head = lax.rem(y + dy + 4, 4) * 2 + lax.rem(core + dc, 2)
-        columns = jnp.dot(
-            u_all[pl.ds(head * 8, 8)].reshape(128, DEPTH),
-            weighted[head],
-            preferred_element_type=F32,
-        )
-        heads[:, pl.ds(pl.multiple_of(head * 128, 128), 128)] = columns.T.astype(BF16)
-
+    o_gather.serve(2, 1)
+    u_gather.line(3)
     project(0, 0)
     u_gather.ring()
-    for turn in range(4):
-        o_gather.ring(turn)
+    o_gather.ring(0)
+    o_gather.ring(1)
+    o_gather.ring(2)
+    o_gather.ring(3)
     project(-1, 0)
     project(1, 0)
+    u_gather.sibling(0)
+    project(0, 1)
+    u_gather.sibling(-1)
+    project(-1, 1)
+    u_gather.sibling(1)
+    project(1, 1)
     u_gather.far()
     project(2, 0)
-    for dy in (0, -1, 1, 2):
-        u_gather.sibling(dy)
-        project(dy, 1)
+    u_gather.sibling(2)
+    project(2, 1)
 
     def partial(target, dst):
         near = target * 8 + half * 4
@@ -543,10 +529,10 @@
             )
 
     low_rows, high_rows = pl.ds(0, 128), pl.ds(128, 128)
-    right, left = (targets[1] * 2 + half, seat), (targets[2] * 2 + half, seat)
+    to_right, to_left = (targets[1] * 2 + half, seat), (targets[2] * 2 + half, seat)
 
     def pass_on(src, dst, slot, target):
-        go(src, dst, p_send.at[slot], p_recv.at[slot], target)
+        remote(src, dst, p_send.at[0], p_recv.at[slot], target).start()
 
     def block(turn, dst):
         o_gather.far(turn)
@@ -554,43 +540,41 @@
         partial(targets[turn], dst)
 
     block(0, part_out.at[0])
-    pass_on(part_out.at[0, low_rows], part_in.at[0, low_rows], 0, right)
-    pass_on(part_out.at[0, high_rows], part_in.at[0, high_rows], 1, left)
+    pass_on(part_out.at[0, low_rows], part_in.at[0, low_rows], 0, to_right)
+    pass_on(part_out.at[0, high_rows], part_in.at[0, high_rows], 1, to_left)
     block(1, part_out.at[1])
-    pass_on(part_out.at[1, high_rows], part_in.at[1, high_rows], 2, right)
+    pass_on(part_out.at[1, high_rows], part_in.at[1, high_rows], 2, to_right)
     block(2, part_out.at[2])
-    pass_on(part_out.at[2, low_rows], part_in.at[2, low_rows], 3, left)
-    landed(part_in.at[0, low_rows], p_send.at[0], p_recv.at[0])
+    pass_on(part_out.at[2, low_rows], part_in.at[2, low_rows], 3, to_left)
+    landed(part_in.at[0, low_rows], p_recv.at[0])
     part_out[1, 0:128] = (
         part_out[1, 0:128].astype(F32) + part_in[0, 0:128].astype(F32)
     ).astype(BF16)
-    pass_on(part_out.at[1, low_rows], part_in.at[1, low_rows], 4, right)
-    landed(part_in.at[0, high_rows], p_send.at[0], p_recv.at[1])
+    pass_on(part_out.at[1, low_rows], part_in.at[1, low_rows], 4, to_right)
+    landed(part_in.at[0, high_rows], p_recv.at[1])
     part_out[2, 128:256] = (
         part_out[2, 128:256].astype(F32) + part_in[0, 128:256].astype(F32)
     ).astype(BF16)
-    pass_on(part_out.at[2, high_rows], part_in.at[2, high_rows], 5, left)
+    pass_on(part_out.at[2, high_rows], part_in.at[2, high_rows], 5, to_left)
     block(3, total)
-    landed(part_in.at[1, high_rows], p_send.at[0], p_recv.at[2])
-    landed(part_in.at[2, low_rows], p_send.at[0], p_recv.at[3])
-    landed(part_in.at[1, low_rows], p_send.at[0], p_recv.at[4])
-    landed(part_in.at[2, high_rows], p_send.at[0], p_recv.at[5])
-    out[...] = total[...] + part_in[1].astype(F32) + part_in[2].astype(F32)
-
-    for copy in sent:
-        copy.wait_send()
+    landed(part_in.at[1, high_rows], p_recv.at[2])
+    landed(part_in.at[2, low_rows], p_recv.at[3])
+    landed(part_in.at[1, low_rows], p_recv.at[4])
+    landed(part_in.at[2, high_rows], p_recv.at[5])
+    offset = bias[...].astype(F32).reshape(1, COLS)
+    out[...] = (
+        total[...] + part_in[1].astype(F32) + part_in[2].astype(F32) + offset
+    ).astype(BF16)
+
     o_gather.finish()
     u_gather.finish()
-
-    @pl.when(swaps)
-    def _():
-        swap.wait_send()
-
+    left(u_in_x, x_sem.at[0])
+    left(table_in, t_sem.at[0])
+    table_copy.wait_send()
+    left(part_out, p_send.at[0])
+    pl.when(swaps)(swap.wait_send)
     for which in range(2):
-
-        @pl.when(jnp.logical_not(here[which]))
-        def _():
-            fold[which].wait_send()
+        pl.when(jnp.logical_not(here[which]))(fold[which].wait_send)
 
 
 def local(
@@ -599,10 +583,10 @@
     vmem = pl.BlockSpec(memory_space=pltpu.VMEM)
     hbm = pl.BlockSpec(memory_space=pl.ANY)
     sems = pltpu.SemaphoreType.DMA
-    summed = pl.pallas_call(
+    return pl.pallas_call(
         kernel,
-        out_shape=jax.ShapeDtypeStruct((TOK, COLS), F32),
-        in_specs=[hbm] * 6 + [vmem],
+        out_shape=jax.ShapeDtypeStruct((TOK, COLS), BF16),
+        in_specs=[hbm] * 6 + [vmem] * 2,
         out_specs=vmem,
         scratch_shapes=[
             pltpu.VMEM((ROWS, TOK), BF16),
@@ -629,18 +613,18 @@
             pltpu.VMEM((3, TOK, COLS), BF16),
             pltpu.VMEM((TOK, COLS), F32),
             sems((8,)),
-            sems((41,)),
+            sems((2,)),
+            sems((16,)),
+            sems((4,)),
+            sems((1,)),
             sems((32,)),
-            sems((63,)),
-            sems((64,)),
+            sems((4,)),
             sems((1,)),
             sems((4,)),
-            sems((4,)),
-            sems((3,)),
-            sems((3,)),
             sems((2,)),
             sems((2,)),
-            sems((6,)),
+            sems((2,)),
+            sems((1,)),
             sems((6,)),
         ],
         compiler_params=pltpu.CompilerParams(
@@ -658,8 +642,8 @@
         value_weight.reshape(COLS, 128),
         out_weight,
         var_mask,
-    )
-    return (summed + out_bias.astype(F32)[None, :]).astype(BF16)
+        out_bias,
+    )
 
 
 def solution(mesh):

time: 78.8 us -> 76.4 us (0.970)
  other arithmetic: 2.46 us -> 0 us
  local copies, waits for them, and re-layouts: 0 us -> 1.67 us
  Pallas kernels: 76.1 us -> 74.6 us
    convert_element_type x2 -> x0, other arithmetic: 2.46 us -> none  [local(): return (summed + out_bias.astype(F32)[None, :]).astype(BF16)]
    unnamed x0 -> x1, local copies, waits for them, and re-layouts: none -> 1.67 us
    pallas_call x1, Pallas kernels: 76.1 us -> 74.6 us  [local(): pl.pallas_call(kernel, out_shape=jax.ShapeDtypeStruct((TOK, COLS), BF16),...]
where the time goes in v5:
time: 76.4 us; the launch traced here: 76.3 us
  Pallas kernels  74.6 us (98%)
  local copies, waits for them, and re-layouts  1.67 us (2%)
    pallas_call x1, Pallas kernels, local(): pl.pallas_call(kernel, out_shape=jax.ShapeDtypeStruct((TOK, COLS), BF16),...  74.6 us
    unnamed x1, local copies, waits for them, and re-layouts  1.67 us

profile of v5, /device:TPU:1, one launch (start us, length us, event | category | flops | bytes accessed | tf_op | source)
XLA Modules:
  0.0 76.3 jit_solution(17283306795916727037)
XLA Ops:
  0.0 74.6 %aggregate.1 = bf16[256,512]{1,0:T(8,128)(2,1)} custom-call(bf16[1536,256]{1,0:T(8,128)(2,1)} %bitcast.5, bf16[1536,512]{1,0:T(8,128)(2,1)} %bitcast.4, bf16[96,512]{1,0:T(8,128)(2,1)} %embed_hbm.1, bf16[32,512]{1,0:T(8,128)(2,1)} %bitcast.7, bf16[512,128]{1,0:T(8,128)(2,1)} %bitcast.6, bf16[512,128]{1,0:T(8,128)(2,1)} %out_weight.1, s32[96]{0:T(128)} %mask.1, ...), custom_call_target="tpu_custom_call" | custom-call | flops 2000000000 | bytes 4000000 | tf_op jit(solution)/shard_map/aggregate/pallas_call | solution.py:586
  74.6 1.7 %copy.10 = bf16[256,512]{1,0:T(8,128)(2,1)} copy(bf16[256,512]{1,0:T(8,128)(2,1)} %aggregate.1) | data formatting | bytes 524288

commit v6 on v5

--- a/solution.py
+++ b/solution.py
@@ -28,9 +28,11 @@
     query_hbm,
     value_hbm,
     out_weight,
+    mask_hbm,
+    bias_hbm,
+    out,
     mask,
     bias,
-    out,
     patches,
     weight,
     embed_pad,
@@ -91,12 +93,15 @@
         pltpu.make_async_copy(query_hbm, left_side.at[pl.ds(128, 32)], l_sem.at[1]),
         pltpu.make_async_copy(embed_hbm, embed_pad.at[pl.ds(0, VARS)], l_sem.at[2]),
     ]
-    for part in range(3):
-        span = pl.ds(part * 512, 512)
-        loads.append(
-            pltpu.make_async_copy(weight_hbm.at[span], weight.at[span], l_sem.at[3 + part])
+    weight_loads = []
+    for part in range(6):
+        span = pl.ds(part * 256, 256)
+        weight_loads.append(
+            pltpu.make_async_copy(weight_hbm.at[span], weight.at[span], l_sem.at[10 + part])
         )
     loads.append(pltpu.make_async_copy(patches_hbm, patches, l_sem.at[6]))
+    loads.append(pltpu.make_async_copy(mask_hbm, mask, l_sem.at[8]))
+    loads.append(pltpu.make_async_copy(bias_hbm, bias, l_sem.at[9]))
 
     swaps = lax.div(y, 2) != half
     swap_to = (x * 2 + 1 - half, (3 - zlo) * 8 + (3 - y) * 2 + core)
@@ -127,7 +132,7 @@
     pl.when(lax.rem(zlo, 3) == 0)(lambda: greet((me, (3 - zlo) * 8 + lane)))
     pl.when(swaps)(lambda: greet(swap_to))
 
-    for copy in loads:
+    for copy in loads[:3] + weight_loads + loads[3:]:
         copy.start()
     stay = pltpu.make_async_copy(out_weight, o_all.at[seat], l_sem.at[7])
 
@@ -313,7 +318,8 @@
     for part in (3, 0, 1, 2):
         wide = 512 if part < 3 else 128
         if part < 3:
-            loads[3 + part].wait()
+            weight_loads[2 * part].wait()
+            weight_loads[2 * part + 1].wait()
             rhs = weight[part * 512 : part * 512 + 512]
         else:
             rhs = embed_pad[...]
@@ -376,25 +382,42 @@
         def _():
             u_in_z[half] = u_mid[which]
 
-    def table_start():
-        for dx in (2, 1, 3):
-            target = lax.rem(x + dx, 4)
-            remote(
-                table_out.at[target],
-                table_in.at[dx - 1],
-                t_sem.at[0],
-                t_sem.at[1],
-                (target * 2 + half, seat),
-            ).start()
-
+    first_core = core == 0
     table_copy = remote(
         table_mid, table_far, t_sem.at[2], t_sem.at[3], (x * 2 + 1 - half, seat)
     )
+    table_share = remote(
+        table, table, t_sem.at[4], t_sem.at[5], device(*turned(0, 0, 1))
+    )
+
+    def table_start():
+        @pl.when(first_core)
+        def _():
+            for dx in (2, 1, 3):
+                target = lax.rem(x + dx, 4)
+                remote(
+                    table_out.at[target],
+                    table_in.at[dx - 1],
+                    t_sem.at[0],
+                    t_sem.at[1],
+                    (target * 2 + half, seat),
+                ).start()
 
     def table_pass():
-        landed(table_in, t_sem.at[1])
-        table_mid[...] = table_out[x] + table_in[0] + table_in[1] + table_in[2]
-        table_copy.start()
+        @pl.when(first_core)
+        def _():
+            landed(table_in, t_sem.at[1])
+            table_mid[...] = table_out[x] + table_in[0] + table_in[1] + table_in[2]
+            table_copy.start()
+
+    def table_end():
+        @pl.when(first_core)
+        def _():
+            table_copy.wait_recv()
+            table[...] = table_mid[...] + table_far[...]
+            table_share.start()
+
+        pl.when(jnp.logical_not(first_core))(table_share.wait_recv)
 
     def reduce_z():
         for source in range(2):
@@ -428,14 +451,14 @@
 
     o_gather.serve(1, 0)
     o_gather.serve(2, 0)
+    u_gather.line(1)
     table_pass()
-    u_gather.line(1)
     o_gather.serve(0, 1)
     o_gather.serve(1, 1)
     u_gather.line(2)
-    loads[6].wait()
-    table_copy.wait_recv()
-    table[...] = table_mid[...] + table_far[...]
+    for copy in loads[3:]:
+        copy.wait()
+    table_end()
     diagonal = lax.div(iota((VAR_CHUNK, CHUNK), 1), PIX) == iota((VAR_CHUNK, CHUNK), 0)
     stacked = HEADS_DEV * VAR_CHUNK
     for chunk in range(ROWS // CHUNK):
@@ -569,8 +592,13 @@
     o_gather.finish()
     u_gather.finish()
     left(u_in_x, x_sem.at[0])
-    left(table_in, t_sem.at[0])
-    table_copy.wait_send()
+
+    @pl.when(first_core)
+    def _():
+        left(table_in, t_sem.at[0])
+        table_copy.wait_send()
+        table_share.wait_send()
+
     left(part_out, p_send.at[0])
     pl.when(swaps)(swap.wait_send)
     for which in range(2):
@@ -586,9 +614,11 @@
     return pl.pallas_call(
         kernel,
         out_shape=jax.ShapeDtypeStruct((TOK, COLS), BF16),
-        in_specs=[hbm] * 6 + [vmem] * 2,
+        in_specs=[hbm] * 8,
         out_specs=vmem,
         scratch_shapes=[
+            pltpu.VMEM((VARS,), jnp.int32),
+            pltpu.VMEM((COLS,), BF16),
             pltpu.VMEM((ROWS, TOK), BF16),
             pltpu.VMEM((ROWS, COLS), BF16),
             pltpu.VMEM((128, COLS), BF16),
@@ -612,7 +642,7 @@
             pltpu.VMEM((3, TOK, COLS), BF16),
             pltpu.VMEM((3, TOK, COLS), BF16),
             pltpu.VMEM((TOK, COLS), F32),
-            sems((8,)),
+            sems((16,)),
             sems((2,)),
             sems((16,)),
             sems((4,)),
@@ -620,7 +650,7 @@
             sems((32,)),
             sems((4,)),
             sems((1,)),
-            sems((4,)),
+            sems((6,)),
             sems((2,)),
             sems((2,)),
             sems((2,)),

time: 76.4 us -> 73.9 us (0.967)
  Pallas kernels: 74.6 us -> 72.1 us
    pallas_call x1, Pallas kernels: 74.6 us -> 72.1 us  [local(): pl.pallas_call(kernel, out_shape=jax.ShapeDtypeStruct((TOK, COLS), BF16),...]
where the time goes in v6:
time: 73.9 us; the launch traced here: 73.8 us
  Pallas kernels  72.1 us (98%)
  local copies, waits for them, and re-layouts  1.67 us (2%)
    pallas_call x1, Pallas kernels, local(): pl.pallas_call(kernel, out_shape=jax.ShapeDtypeStruct((TOK, COLS), BF16),...  72.1 us
    unnamed x1, local copies, waits for them, and re-layouts  1.67 us

profile of v6, /device:TPU:1, one launch (start us, length us, event | category | flops | bytes accessed | tf_op | source)
XLA Modules:
  0.0 73.8 jit_solution(16192594034138150046)
XLA Ops:
  0.0 72.1 %aggregate.1 = bf16[256,512]{1,0:T(8,128)(2,1)} custom-call(bf16[1536,256]{1,0:T(8,128)(2,1)} %bitcast.5, bf16[1536,512]{1,0:T(8,128)(2,1)} %bitcast.4, bf16[96,512]{1,0:T(8,128)(2,1)} %embed_hbm.1, bf16[32,512]{1,0:T(8,128)(2,1)} %bitcast.7, bf16[512,128]{1,0:T(8,128)(2,1)} %bitcast.6, bf16[512,128]{1,0:T(8,128)(2,1)} %out_weight.1, s32[96]{0:T(128)} %mask_hbm.1, ...), custom_call_target="tpu_custom_call" | custom-call | flops 2000000000 | bytes 4000000 | tf_op jit(solution)/shard_map/aggregate/pallas_call | solution.py:614
  72.1 1.7 %copy.10 = bf16[256,512]{1,0:T(8,128)(2,1)} copy(bf16[256,512]{1,0:T(8,128)(2,1)} %aggregate.1) | data formatting | bytes 524288

commit v7 on v6

--- a/solution.py
+++ b/solution.py
@@ -439,8 +439,9 @@
         )
         heads[:, pl.ds(pl.multiple_of(head * 128, 128), 128)] = columns.T.astype(BF16)
 
+    o_gather.serve(0, 0)
     table_start()
-    o_gather.serve(0, 0)
+    o_gather.serve(1, 0)
     reduce_z()
     u_gather.own()
 
@@ -449,7 +450,6 @@
         o_gather.arrive(turned(0, 0))
         o_gather.own()
 
-    o_gather.serve(1, 0)
     o_gather.serve(2, 0)
     u_gather.line(1)
     table_pass()
@@ -514,12 +514,12 @@
 
     o_gather.serve(2, 1)
     u_gather.line(3)
-    project(0, 0)
     u_gather.ring()
     o_gather.ring(0)
     o_gather.ring(1)
     o_gather.ring(2)
     o_gather.ring(3)
+    project(0, 0)
     project(-1, 0)
     project(1, 0)
     u_gather.sibling(0)

time: 73.9 us -> 73.9 us (level)
  no operation moved by 1% of the time
where the time goes in v7:
time: 73.9 us; the launch traced here: 73.8 us
  Pallas kernels  72.1 us (98%)
  local copies, waits for them, and re-layouts  1.67 us (2%)
    pallas_call x1, Pallas kernels, local(): pl.pallas_call(kernel, out_shape=jax.ShapeDtypeStruct((TOK, COLS), BF16),...  72.1 us
    unnamed x1, local copies, waits for them, and re-layouts  1.67 us

profile of v7, /device:TPU:1, one launch (start us, length us, event | category | flops | bytes accessed | tf_op | source)
XLA Modules:
  0.0 73.8 jit_solution(10980562483450905306)
XLA Ops:
  0.0 72.1 %aggregate.1 = bf16[256,512]{1,0:T(8,128)(2,1)} custom-call(bf16[1536,256]{1,0:T(8,128)(2,1)} %bitcast.5, bf16[1536,512]{1,0:T(8,128)(2,1)} %bitcast.4, bf16[96,512]{1,0:T(8,128)(2,1)} %embed_hbm.1, bf16[32,512]{1,0:T(8,128)(2,1)} %bitcast.7, bf16[512,128]{1,0:T(8,128)(2,1)} %bitcast.6, bf16[512,128]{1,0:T(8,128)(2,1)} %out_weight.1, s32[96]{0:T(128)} %mask_hbm.1, ...), custom_call_target="tpu_custom_call" | custom-call | flops 2000000000 | bytes 4000000 | tf_op jit(solution)/shard_map/aggregate/pallas_call | solution.py:614
  72.1 1.7 %copy.10 = bf16[256,512]{1,0:T(8,128)(2,1)} copy(bf16[256,512]{1,0:T(8,128)(2,1)} %aggregate.1) | data formatting | bytes 524288

commit v8 on v6

--- a/solution.py
+++ b/solution.py
@@ -103,6 +103,9 @@
     loads.append(pltpu.make_async_copy(mask_hbm, mask, l_sem.at[8]))
     loads.append(pltpu.make_async_copy(bias_hbm, bias, l_sem.at[9]))
 
+    for copy in loads[:3] + weight_loads + loads[3:]:
+        copy.start()
+
     swaps = lax.div(y, 2) != half
     swap_to = (x * 2 + 1 - half, (3 - zlo) * 8 + (3 - y) * 2 + core)
     fold_seat = x * 8 + lane
@@ -132,8 +135,6 @@
     pl.when(lax.rem(zlo, 3) == 0)(lambda: greet((me, (3 - zlo) * 8 + lane)))
     pl.when(swaps)(lambda: greet(swap_to))
 
-    for copy in loads[:3] + weight_loads + loads[3:]:
-        copy.start()
     stay = pltpu.make_async_copy(out_weight, o_all.at[seat], l_sem.at[7])
 
     @pl.when(jnp.logical_not(swaps))

time: 73.9 us -> 74 us (level)
  no operation moved by 1% of the time
where the time goes in v8:
time: 74 us; the launch traced here: 73.9 us
  Pallas kernels  72.2 us (98%)
  local copies, waits for them, and re-layouts  1.67 us (2%)
    pallas_call x1, Pallas kernels, local(): pl.pallas_call(kernel, out_shape=jax.ShapeDtypeStruct((TOK, COLS), BF16),...  72.2 us
    unnamed x1, local copies, waits for them, and re-layouts  1.67 us

profile of v8, /device:TPU:1, one launch (start us, length us, event | category | flops | bytes accessed | tf_op | source)
XLA Modules:
  0.0 73.9 jit_solution(14337254083662119766)
XLA Ops:
  0.0 72.2 %aggregate.1 = bf16[256,512]{1,0:T(8,128)(2,1)} custom-call(bf16[1536,256]{1,0:T(8,128)(2,1)} %bitcast.5, bf16[1536,512]{1,0:T(8,128)(2,1)} %bitcast.4, bf16[96,512]{1,0:T(8,128)(2,1)} %embed_hbm.1, bf16[32,512]{1,0:T(8,128)(2,1)} %bitcast.7, bf16[512,128]{1,0:T(8,128)(2,1)} %bitcast.6, bf16[512,128]{1,0:T(8,128)(2,1)} %out_weight.1, s32[96]{0:T(128)} %mask_hbm.1, ...), custom_call_target="tpu_custom_call" | custom-call | flops 2000000000 | bytes 4000000 | tf_op jit(solution)/shard_map/aggregate/pallas_call | solution.py:615
  72.2 1.7 %copy.10 = bf16[256,512]{1,0:T(8,128)(2,1)} copy(bf16[256,512]{1,0:T(8,128)(2,1)} %aggregate.1) | data formatting | bytes 524288
